TPU v7x, 512 devices: a whole 4x8x8 slice. The times are simulated.
512 devices in a mesh: row: 32 (over y, z_hi, core), col: 16 (over z_lo, x).
Axes of the slice: x: 4, y: 8, z: 8 (z_hi: 2, z_lo: 4; z = z_hi * 4 + z_lo), core: 2. Of those that a mesh axis runs over, the one named last changes fastest.
Arguments:
- queries: bfloat16 [512, 128, 1536], P('row', 'col'), may hold values from -8 to 8
- keys: bfloat16 [512, 128, 1536], P('row', 'col'), may hold values from -8 to 8
- values: bfloat16 [512, 128, 1536], P('row', 'col'), may hold values from -6 to 6
- out_grad: bfloat16 [512, 128, 1536], P('row', 'col'), may hold values from -15 to 15
Outputs:
- qkv_grad: bfloat16 [512, 128, 4608], P('row', 'col')
All inputs are finite; a program needn't handle non-finite values.
Results may differ from a plain program's by a relative error of at most 0.007.
Values may be sent and summed in bfloat16 or wider, within the bound.
A program may use at most 128 MiB of HBM per device.

v0:
```python
import math

import jax
import jax.numpy as jnp
from jax import lax
from jax.sharding import PartitionSpec as P

HEAD_DIM = 128
RADIUS = 8


FLOOR = -1e30
band_height = 8


def padded(block, sides, width):
    for axis, dim in sides:
        count = lax.axis_size(axis)
        forward = [(i, i + 1) for i in range(count - 1)]
        backward = [(target, source) for source, target in forward]
        low = lax.ppermute(
            lax.slice_in_dim(block, block.shape[dim] - width, None, axis=dim), axis, forward
        )
        high = lax.ppermute(lax.slice_in_dim(block, 0, width, axis=dim), axis, backward)
        block = jnp.concatenate([low, block, high], axis=dim)
    return block


def pair_mask(query_rows, query_cols, key_rows, key_cols, grid_rows, grid_cols):
    query_row_in = (query_rows >= 0) & (query_rows < grid_rows)
    query_col_in = (query_cols >= 0) & (query_cols < grid_cols)
    key_row_in = (key_rows >= 0) & (key_rows < grid_rows)
    key_col_in = (key_cols >= 0) & (key_cols < grid_cols)
    row_match = (
        (jnp.abs(query_rows[:, None] - key_rows[None, :]) <= RADIUS)
        & query_row_in[:, None]
        & key_row_in[None, :]
    )
    col_match = (
        (jnp.abs(query_cols[:, None] - key_cols[None, :]) <= RADIUS)
        & query_col_in[:, None]
        & key_col_in[None, :]
    )
    joined = row_match[:, None, :, None] & col_match[None, :, None, :]
    return joined.reshape(
        query_rows.shape[0] * query_cols.shape[0], key_rows.shape[0] * key_cols.shape[0]
    )


def split_heads(block):
    return block.reshape(-1, block.shape[-1] // HEAD_DIM, HEAD_DIM)


def to_grid(stat, tile_rows, tile_cols):
    return jnp.transpose(stat[:, :, 0]).reshape(tile_rows, tile_cols, -1)


def query_terms(query_heads, key_heads, value_heads, grad_heads, mask, scale_factor):
    scores = (
        jnp.einsum("qhd,khd->hqk", query_heads, key_heads, preferred_element_type=jnp.float32)
        * scale_factor
    )
    masked = jnp.where(mask[None], scores, FLOOR)
    peak = jnp.max(masked, axis=2, keepdims=True)
    log_total = peak + jnp.log(jnp.sum(jnp.exp(masked - peak), axis=2, keepdims=True))
    weights = jnp.exp(masked - log_total)
    grad_prob = jnp.einsum(
        "qhd,khd->hqk", grad_heads, value_heads, preferred_element_type=jnp.float32
    )
    offset = jnp.sum(weights * grad_prob, axis=2, keepdims=True)
    grad_score = (weights * (grad_prob - offset)).astype(jnp.bfloat16)
    return (weights, grad_score, log_total, offset)


def key_terms(
    query_heads, grad_heads, log_total, offset, key_heads, value_heads, mask, scale_factor
):
    scores = (
        jnp.einsum("qhd,khd->hqk", query_heads, key_heads, preferred_element_type=jnp.float32)
        * scale_factor
    )
    masked = jnp.where(mask[None], scores, FLOOR)
    weights = jnp.exp(masked - log_total)
    grad_prob = jnp.einsum(
        "qhd,khd->hqk", grad_heads, value_heads, preferred_element_type=jnp.float32
    )
    grad_score = (weights * (grad_prob - offset)).astype(jnp.bfloat16)
    key_grad = (
        jnp.einsum("hqk,qhd->khd", grad_score, query_heads, preferred_element_type=jnp.float32)
        * scale_factor
    )
    value_grad = jnp.einsum(
        "hqk,qhd->khd", weights.astype(jnp.bfloat16), grad_heads, preferred_element_type=jnp.float32
    )
    return (key_grad, value_grad)


def per_device(queries, keys, values, out_grad):
    tile_rows, tile_cols, channels = queries.shape
    head_count = channels // HEAD_DIM
    scale_factor = 1.0 / math.sqrt(HEAD_DIM)
    grid_rows = tile_rows * lax.axis_size("row")
    grid_cols = tile_cols * lax.axis_size("col")
    row_start = lax.axis_index("row") * tile_rows
    col_start = lax.axis_index("col") * tile_cols
    own_cols = col_start + jnp.arange(tile_cols, dtype=jnp.int32)
    outer_cols = col_start - RADIUS + jnp.arange(tile_cols + 2 * RADIUS, dtype=jnp.int32)
    paired = jnp.concatenate([keys, values], axis=2)
    beside_all = padded(paired, (("row", 0), ("col", 1)), RADIUS)

    def query_band(start, rows):
        query_block = lax.dynamic_slice_in_dim(queries, start, rows, 0)
        grad_block = lax.dynamic_slice_in_dim(out_grad, start, rows, 0)
        reach_block = lax.dynamic_slice_in_dim(beside_all, start, rows + 2 * RADIUS, 0)
        band_rows = row_start + start + jnp.arange(rows, dtype=jnp.int32)
        reach_rows = row_start + start - RADIUS + jnp.arange(rows + 2 * RADIUS, dtype=jnp.int32)
        mask = pair_mask(band_rows, own_cols, reach_rows, outer_cols, grid_rows, grid_cols)
        key_heads = split_heads(reach_block[:, :, :channels])
        value_heads = split_heads(reach_block[:, :, channels:])
        query_heads = split_heads(query_block)
        grad_heads = split_heads(grad_block)
        weights, grad_score, log_total, offset = query_terms(
            query_heads, key_heads, value_heads, grad_heads, mask, scale_factor
        )
        query_grad = (
            jnp.einsum("hqk,khd->qhd", grad_score, key_heads, preferred_element_type=jnp.float32)
            * scale_factor
        )
        query_grad = query_grad.astype(jnp.bfloat16).reshape(rows, tile_cols, channels)
        return (query_grad, weights, grad_score, log_total, offset, query_heads, grad_heads)

    starts = jnp.arange(tile_rows // band_height, dtype=jnp.int32) * band_height

    def query_step(start):
        query_grad, weights, grad_score, log_total, offset, query_heads, grad_heads = query_band(
            start, band_height
        )
        stats = jnp.concatenate(
            [to_grid(log_total, band_height, tile_cols), to_grid(offset, band_height, tile_cols)],
            axis=2,
        )
        return (query_grad, stats)

    query_grads, stat_bands = lax.map(query_step, starts)
    query_grad = query_grads.reshape(tile_rows, tile_cols, channels)
    stats = stat_bands.reshape(tile_rows, tile_cols, 2 * head_count)
    query_pair = jnp.concatenate([queries, out_grad], axis=2)
    query_around = padded(query_pair, (("row", 0), ("col", 1)), RADIUS)
    stat_around = padded(stats, (("row", 0), ("col", 1)), RADIUS)

    def key_step(start):
        key_block = lax.dynamic_slice_in_dim(keys, start, band_height, 0)
        value_block = lax.dynamic_slice_in_dim(values, start, band_height, 0)
        reach_pair = lax.dynamic_slice_in_dim(query_around, start, band_height + 2 * RADIUS, 0)
        reach_stats = lax.dynamic_slice_in_dim(stat_around, start, band_height + 2 * RADIUS, 0)
        band_rows = row_start + start + jnp.arange(band_height, dtype=jnp.int32)
        reach_rows = (
            row_start + start - RADIUS + jnp.arange(band_height + 2 * RADIUS, dtype=jnp.int32)
        )
        key_mask = pair_mask(reach_rows, outer_cols, band_rows, own_cols, grid_rows, grid_cols)
        flat_stats = reach_stats.reshape(-1, 2 * head_count)
        outer_total = jnp.transpose(flat_stats[:, :head_count])[:, :, None]
        outer_offset = jnp.transpose(flat_stats[:, head_count:])[:, :, None]
        key_grad, value_grad = key_terms(
            split_heads(reach_pair[:, :, :channels]),
            split_heads(reach_pair[:, :, channels:]),
            outer_total,
            outer_offset,
            split_heads(key_block),
            split_heads(value_block),
            key_mask,
            scale_factor,
        )
        return (
            key_grad.astype(jnp.bfloat16).reshape(band_height, tile_cols, channels),
            value_grad.astype(jnp.bfloat16).reshape(band_height, tile_cols, channels),
        )

    key_bands, value_bands = lax.map(key_step, starts)
    key_grad = key_bands.reshape(tile_rows, tile_cols, channels)
    value_grad = value_bands.reshape(tile_rows, tile_cols, channels)
    return jnp.concatenate([query_grad, key_grad, value_grad], axis=2)


def solution(mesh):
    return jax.shard_map(
        per_device,
        mesh=mesh,
        in_specs=(
            P("row", "col", None),
            P("row", "col", None),
            P("row", "col", None),
            P("row", "col", None),
        ),
        out_specs=P("row", "col", None),
        check_vma=False,
    )
```

profile of v0, /device:TPU:113, one launch (start us, length us, event | category | flops | bytes accessed | tf_op | source)
XLA Modules:
  0.0 257.6 jit_solution(13455511632197177565)
XLA Ops:
  2.1 10.3 %collective-permute-start = (bf16[8,8,3072]{2,1,0:T(8,128)(2,1)S(1)}, bf16[8,8,3072]{2,1,0:T(8,128)(2,1)S(1)}, u32[]{:S(2)}, u32[]{:S(2)}) collective-permute-start(bf16[8,8,3072]{2,1,0:T(8,128)(2,1)S(1)} %get-tuple-element.407), channel_id=1, source_target_pairs={{0,16},{16,32},{32,48},{48,64},{64,80},{80,96},{96,112},{112,128},... | collective-permute-start | bytes 1179656 | tf_op jit(solution)/shard_map/ppermute | solution.py:21
  15.4 15.6 %collective-permute-done = bf16[8,8,3072]{2,1,0:T(8,128)(2,1)S(1)} collective-permute-done((bf16[8,8,3072]{2,1,0:T(8,128)(2,1)S(1)}, bf16[8,8,3072]{2,1,0:T(8,128)(2,1)S(1)}, u32[]{:S(2)}, u32[]{:S(2)}) %collective-permute-start) | collective-permute-done | bytes 393248 | tf_op jit(solution)/shard_map/ppermute | solution.py:21
  32.4 3.1 %collective-permute-start.2 = (bf16[32,8,3072]{2,1,0:T(8,128)(2,1)}, bf16[32,8,3072]{2,1,0:T(8,128)(2,1)}, u32[]{:S(2)}, u32[]{:S(2)}) collective-permute-start(bf16[32,8,3072]{2,1,0:T(8,128)(2,1)} %pad_maximum_fusion.2), channel_id=1, source_target_pairs={{0,1},{1,2},{2,3},{3,4},{4,5},{5,6},{6,7},{7,8},{8,9},{9,10},{10,1... | collective-permute-start | bytes 4718600 | tf_op jit(solution)/shard_map/ppermute | solution.py:21
  35.5 4.3 %collective-permute-start.3 = (bf16[32,8,3072]{2,1,0:T(8,128)(2,1)}, bf16[32,8,3072]{2,1,0:T(8,128)(2,1)}, u32[]{:S(2)}, u32[]{:S(2)}) collective-permute-start(bf16[32,8,3072]{2,1,0:T(8,128)(2,1)} %pad_maximum_fusion.2), channel_id=1, source_target_pairs={{1,0},{2,1},{3,2},{4,3},{5,4},{6,5},{7,6},{8,7},{9,8},{10,9},{11,1... | collective-permute-start | bytes 4718600 | tf_op jit(solution)/shard_map/ppermute | solution.py:24
  41.8 8.9 %collective-permute-start.4 = (bf16[8,8,3072]{2,1,0:T(8,128)(2,1)}, bf16[8,8,3072]{2,1,0:T(8,128)(2,1)S(1)}, u32[]{:S(2)}, u32[]{:S(2)}) collective-permute-start(bf16[8,8,3072]{2,1,0:T(8,128)(2,1)} %get-tuple-element.409), channel_id=1, source_target_pairs={{0,16},{16,32},{32,48},{48,64},{64,80},{80,96},{96,112},{112,128},... | collective-permute-start | bytes 1179656 | tf_op jit(solution)/shard_map/ppermute | solution.py:21
  52.7 42.0 %collective-permute-done.4 = bf16[8,8,3072]{2,1,0:T(8,128)(2,1)S(1)} collective-permute-done((bf16[8,8,3072]{2,1,0:T(8,128)(2,1)}, bf16[8,8,3072]{2,1,0:T(8,128)(2,1)S(1)}, u32[]{:S(2)}, u32[]{:S(2)}) %collective-permute-start.4) | collective-permute-done | bytes 393248 | tf_op jit(solution)/shard_map/ppermute | solution.py:21
  94.6 6.4 %collective-permute-done.5 = bf16[8,8,3072]{2,1,0:T(8,128)(2,1)S(1)} collective-permute-done((bf16[8,8,3072]{2,1,0:T(8,128)(2,1)}, bf16[8,8,3072]{2,1,0:T(8,128)(2,1)S(1)}, u32[]{:S(2)}, u32[]{:S(2)}) %collective-permute-start.5) | collective-permute-done | bytes 393248 | tf_op jit(solution)/shard_map/ppermute | solution.py:24
  104.4 5.5 %collective-permute-start.7 = (bf16[32,8,3072]{2,1,0:T(8,128)(2,1)}, bf16[32,8,3072]{2,1,0:T(8,128)(2,1)}, u32[]{:S(2)}, u32[]{:S(2)}) collective-permute-start(bf16[32,8,3072]{2,1,0:T(8,128)(2,1)} %pad_maximum_fusion.3), channel_id=1, source_target_pairs={{1,0},{2,1},{3,2},{4,3},{5,4},{6,5},{7,6},{8,7},{9,8},{10,9},{11,1... | collective-permute-start | bytes 4718600 | tf_op jit(solution)/shard_map/ppermute | solution.py:24
  109.9 4.7 %pad_maximum_fusion = bf16[32,24,3072]{2,1,0:T(8,128)(2,1)} fusion(bf16[32,8,3072]{2,1,0:T(8,128)(2,1)} %collective-permute-done.3, bf16[8,8,3072]{2,1,0:T(8,128)(2,1)S(1)} %collective-permute-done.1, bf16[16,8,3072]{2,1,0:T(8,128)(2,1)S(1)} %constant_dynamic-update-slice_fusion.3, bf16[8,8,3072]{2,1,0:T(8,128)(2,1)S(1)} %collective-permute-done, ...), kind=kLoop, calls=%fused_computation.85 | loop fusion | flops 23592960 | bytes 9437184 | tf_op jit(solution)/shard_map/concatenate | solution.py:25
  115.3 58.8 %while.30 = (s32[]{:T(128)}, bf16[2,8,8,1536]{3,2,1,0:T(8,128)(2,1)}, f32[2,8,8,24]{3,2,1,0:T(8,128)S(1)}, s32[2]{0:T(128)S(1)}, bf16[32,24,3072]{2,1,0:T(8,128)...) while((s32[]{:T(128)}, ...), condition=%wide.region_4.5_spmd.clone, body=%wide.region_0.4_spmd.clone.sunk | while | flops 345282752 | bytes 33714352 | solution.py:144
  119.2 3.5 %constant_dynamic-slice_fusion.15 = (bf16[24,24,1536]{2,1,0:T(8,128)(2,1)}, bf16[24,24,1536]{2,1,0:T(8,128)(2,1)S(1)}) fusion(bf16[32,24,3072]{2,1,0:T(8,128)(2,1)} %get-tuple-element.613, s32[]{:T(128)S(6)} %select_n.54, s32[]{:T(128)S(6)} %add.328), kind=kLoop, calls=%fused_computation.39.clone.1 | loop fusion | bytes 7077896 | tf_op jit(solution)/shard_map/while/body/eval_jaxpr/slice | solution.py:119
  127.9 2.9 %fusion.91 = (f32[12,64]{1,0:T(8,128)S(1)}, f32[12,64,576]{2,1,0:T(8,128)S(1)}) fusion(bf16[576,12,128]{2,1,0:T(8,128)(2,1)} %reshape.458, bf16[64,12,128]{2,1,0:T(8,128)(2,1)S(1)} %reshape.459, pred[64,576]{1,0:T(8,128)(4,1)S(1)} %and.365), kind=kOutput, calls=%fused_computation.99.clone.1 | convolution fusion | flops 114572544 | bytes 3775488 | tf_op jit(solution)/shard_map/while/body/eval_jaxpr/qhd,khd->hqk/dot_general | solution.py:60
  131.5 4.3 %reshape.460 = bf16[576,12,128]{2,1,0:T(8,128)(2,1)} reshape(bf16[24,24,1536]{2,1,0:T(8,128)(2,1)} %get-tuple-element.556) | data formatting | bytes 3538944 | tf_op jit(solution)/shard_map/while/body/eval_jaxpr/reshape | solution.py:51
  135.8 4.1 %multiply_reduce_fusion.2 = (f32[12,64]{1,0:T(8,128)S(1)}, f32[12,64,576]{2,1,0:T(8,128)}) fusion(f32[12,64,576]{2,1,0:T(8,128)S(1)} %get-tuple-element.554, f32[12,64]{1,0:T(8,128)S(1)} %log_add_fusion.2, bf16[576,12,128]{2,1,0:T(8,128)(2,1)} %reshape.460, bf16[64,12,128]{2,1,0:T(8,128)(2,1)S(1)} %reshape.461), kind=kOutput, calls=%fused_computation.5.clone.1 | convolution fusion | flops 114572544 | bytes 5511168 | tf_op jit(solution)/shard_map/while/body/eval_jaxpr/qhd,khd->hqk/dot_general | solution.py:67
  140.2 3.5 %fusion.92 = bf16[64,12,128]{2,0,1:T(8,128)(2,1)S(1)} fusion(bf16[576,12,128]{2,1,0:T(8,128)(2,1)} %reshape.458, f32[12,64,576]{2,1,0:T(8,128)} %get-tuple-element.558, f32[12,64,576]{2,1,0:T(8,128)S(1)} %get-tuple-element.554, f32[12,64]{1,0:T(8,128)S(1)} %get-tuple-element.559, f32[12,64]{1,0:T(8,128)S(1)} %log_add_fusion.2), kind=kOutput, calls=%fused_computation.16.clone.1 | convolution fusion | flops 115212288 | bytes 5511168 | tf_op jit(solution)/shard_map/while/body/eval_jaxpr/hqk,khd->qhd/dot_general | solution.py:126
  148.6 3.5 %constant_dynamic-slice_fusion.15 = (bf16[24,24,1536]{2,1,0:T(8,128)(2,1)}, bf16[24,24,1536]{2,1,0:T(8,128)(2,1)S(1)}) fusion(bf16[32,24,3072]{2,1,0:T(8,128)(2,1)} %get-tuple-element.613, s32[]{:T(128)S(6)} %select_n.54, s32[]{:T(128)S(6)} %add.328), kind=kLoop, calls=%fused_computation.39.clone.1 | loop fusion | bytes 7077896 | tf_op jit(solution)/shard_map/while/body/eval_jaxpr/slice | solution.py:119
  157.3 2.9 %fusion.91 = (f32[12,64]{1,0:T(8,128)S(1)}, f32[12,64,576]{2,1,0:T(8,128)S(1)}) fusion(bf16[576,12,128]{2,1,0:T(8,128)(2,1)} %reshape.458, bf16[64,12,128]{2,1,0:T(8,128)(2,1)S(1)} %reshape.459, pred[64,576]{1,0:T(8,128)(4,1)S(1)} %and.365), kind=kOutput, calls=%fused_computation.99.clone.1 | convolution fusion | flops 114572544 | bytes 3775488 | tf_op jit(solution)/shard_map/while/body/eval_jaxpr/qhd,khd->hqk/dot_general | solution.py:60
  160.9 4.3 %reshape.460 = bf16[576,12,128]{2,1,0:T(8,128)(2,1)} reshape(bf16[24,24,1536]{2,1,0:T(8,128)(2,1)} %get-tuple-element.556) | data formatting | bytes 3538944 | tf_op jit(solution)/shard_map/while/body/eval_jaxpr/reshape | solution.py:51
  165.2 4.1 %multiply_reduce_fusion.2 = (f32[12,64]{1,0:T(8,128)S(1)}, f32[12,64,576]{2,1,0:T(8,128)}) fusion(f32[12,64,576]{2,1,0:T(8,128)S(1)} %get-tuple-element.554, f32[12,64]{1,0:T(8,128)S(1)} %log_add_fusion.2, bf16[576,12,128]{2,1,0:T(8,128)(2,1)} %reshape.460, bf16[64,12,128]{2,1,0:T(8,128)(2,1)S(1)} %reshape.461), kind=kOutput, calls=%fused_computation.5.clone.1 | convolution fusion | flops 114572544 | bytes 5511168 | tf_op jit(solution)/shard_map/while/body/eval_jaxpr/qhd,khd->hqk/dot_general | solution.py:67
  169.6 3.5 %fusion.92 = bf16[64,12,128]{2,0,1:T(8,128)(2,1)S(1)} fusion(bf16[576,12,128]{2,1,0:T(8,128)(2,1)} %reshape.458, f32[12,64,576]{2,1,0:T(8,128)} %get-tuple-element.558, f32[12,64,576]{2,1,0:T(8,128)S(1)} %get-tuple-element.554, f32[12,64]{1,0:T(8,128)S(1)} %get-tuple-element.559, f32[12,64]{1,0:T(8,128)S(1)} %log_add_fusion.2), kind=kOutput, calls=%fused_computation.16.clone.1 | convolution fusion | flops 115212288 | bytes 5511168 | tf_op jit(solution)/shard_map/while/body/eval_jaxpr/hqk,khd->qhd/dot_general | solution.py:126
  174.3 2.7 %collective-permute-start.8 = (f32[8,8,24]{0,2,1:T(8,128)S(1)}, f32[8,8,24]{0,2,1:T(8,128)S(1)}, u32[]{:S(2)}, u32[]{:S(2)}) collective-permute-start(f32[8,8,24]{0,2,1:T(8,128)S(1)} %get-tuple-element.411), channel_id=1, source_target_pairs={{0,16},{16,32},{32,48},{48,64},{64,80},{80,96},{96,112},{112,128},... | collective-permute-start | bytes 18440 | tf_op jit(solution)/shard_map/ppermute | solution.py:21
  179.0 7.8 %collective-permute-done.9 = f32[8,8,24]{0,2,1:T(8,128)S(1)} collective-permute-done((f32[8,8,24]{0,2,1:T(8,128)S(1)}, f32[8,8,24]{0,2,1:T(8,128)S(1)}, u32[]{:S(2)}, u32[]{:S(2)}) %collective-permute-start.9) | collective-permute-done | bytes 6176 | tf_op jit(solution)/shard_map/ppermute | solution.py:24
  188.9 5.7 %collective-permute-start.11 = (f32[32,8,24]{0,2,1:T(8,128)S(1)}, f32[32,8,24]{0,2,1:T(8,128)S(1)}, u32[]{:S(2)}, u32[]{:S(2)}) collective-permute-start(f32[32,8,24]{0,2,1:T(8,128)S(1)} %pad_maximum_fusion.6), channel_id=1, source_target_pairs={{1,0},{2,1},{3,2},{4,3},{5,4},{6,5},{7,6},{8,7},{9,8},{10,9},{11,1... | collective-permute-start | bytes 73736 | tf_op jit(solution)/shard_map/ppermute | solution.py:24
  194.6 5.1 %pad_maximum_fusion.1 = bf16[32,24,3072]{2,1,0:T(8,128)(2,1)} fusion(bf16[32,8,3072]{2,1,0:T(8,128)(2,1)} %collective-permute-done.7, bf16[8,8,3072]{2,1,0:T(8,128)(2,1)} %copy-done.3, bf16[16,8,3072]{2,1,0:T(8,128)(2,1)S(1)} %constant_dynamic-update-slice_fusion.5, bf16[8,8,3072]{2,1,0:T(8,128)(2,1)} %copy-done.2, ...), kind=kLoop, calls=%fused_computation.86 | loop fusion | flops 23592960 | bytes 9437184 | tf_op jit(solution)/shard_map/concatenate | solution.py:25
  201.3 54.0 %while.31 = (s32[]{:T(128)}, bf16[2,8,8,1536]{3,2,1,0:T(8,128)(2,1)}, bf16[2,8,8,1536]{3,2,1,0:T(8,128)(2,1)}, s32[2]{0:T(128)S(1)}, bf16[32,24,3072]{2,1,0:T(8,...) while((s32[]{:T(128)}, ...), condition=%wide.region_6.7_spmd.clone, body=%wide.region_5.6_spmd.clone.sunk | while | flops 456415424 | bytes 40558836 | solution.py:179
  205.3 3.5 %constant_dynamic-slice_fusion.17 = (bf16[24,24,1536]{2,1,0:T(8,128)(2,1)}, bf16[24,24,1536]{2,1,0:T(8,128)(2,1)S(1)}) fusion(bf16[32,24,3072]{2,1,0:T(8,128)(2,1)} %get-tuple-element.663, s32[]{:T(128)S(6)} %select_n.57, s32[]{:T(128)S(6)} %add.349), kind=kLoop, calls=%fused_computation.80.clone.1 | loop fusion | bytes 7077896 | tf_op jit(solution)/shard_map/while/body/eval_jaxpr/slice | solution.py:166
  217.1 3.1 %reshape.462 = bf16[576,12,128]{2,1,0:T(8,128)(2,1)S(1)} reshape(bf16[24,24,1536]{2,1,0:T(8,128)(2,1)} %get-tuple-element.571) | data formatting | bytes 3538944 | tf_op jit(solution)/shard_map/while/body/eval_jaxpr/reshape | solution.py:51
  220.4 4.1 %fusion.104 = bf16[64,12,128]{2,0,1:T(8,128)(2,1)S(1)} fusion(bf16[576,12,128]{2,1,0:T(8,128)(2,1)} %reshape.463, f32[12,576,64]{1,2,0:T(8,128)} %subtract_exponential_fusion.3, bf16[576,12,128]{2,1,0:T(8,128)(2,1)S(1)} %reshape.462, f32[12,576]{1,0:T(8,128)S(1)} %get-tuple-element.574, bf16[64,12,128]{2,1,0:T(8,128)(2,1)S(1)} %reshape.466), kind=kOutput, calls=%fused_computation.56.clone.1 | convolution fusion | flops 228016128 | bytes 5729280 | tf_op jit(solution)/shard_map/while/body/eval_jaxpr/hqk,qhd->khd/dot_general | solution.py:89
  232.3 3.5 %constant_dynamic-slice_fusion.17 = (bf16[24,24,1536]{2,1,0:T(8,128)(2,1)}, bf16[24,24,1536]{2,1,0:T(8,128)(2,1)S(1)}) fusion(bf16[32,24,3072]{2,1,0:T(8,128)(2,1)} %get-tuple-element.663, s32[]{:T(128)S(6)} %select_n.57, s32[]{:T(128)S(6)} %add.349), kind=kLoop, calls=%fused_computation.80.clone.1 | loop fusion | bytes 7077896 | tf_op jit(solution)/shard_map/while/body/eval_jaxpr/slice | solution.py:166
  235.8 2.6 %reshape.463 = bf16[576,12,128]{2,1,0:T(8,128)(2,1)} reshape(bf16[24,24,1536]{2,1,0:T(8,128)(2,1)S(1)} %get-tuple-element.572) | data formatting | bytes 3538944 | tf_op jit(solution)/shard_map/while/body/eval_jaxpr/reshape | solution.py:51
  244.1 3.1 %reshape.462 = bf16[576,12,128]{2,1,0:T(8,128)(2,1)S(1)} reshape(bf16[24,24,1536]{2,1,0:T(8,128)(2,1)} %get-tuple-element.571) | data formatting | bytes 3538944 | tf_op jit(solution)/shard_map/while/body/eval_jaxpr/reshape | solution.py:51
  247.4 4.1 %fusion.104 = bf16[64,12,128]{2,0,1:T(8,128)(2,1)S(1)} fusion(bf16[576,12,128]{2,1,0:T(8,128)(2,1)} %reshape.463, f32[12,576,64]{1,2,0:T(8,128)} %subtract_exponential_fusion.3, bf16[576,12,128]{2,1,0:T(8,128)(2,1)S(1)} %reshape.462, f32[12,576]{1,0:T(8,128)S(1)} %get-tuple-element.574, bf16[64,12,128]{2,1,0:T(8,128)(2,1)S(1)} %reshape.466), kind=kOutput, calls=%fused_computation.56.clone.1 | convolution fusion | flops 228016128 | bytes 5729280 | tf_op jit(solution)/shard_map/while/body/eval_jaxpr/hqk,qhd->khd/dot_general | solution.py:89
  (147 shorter events, 58.2 us)
Async XLA Ops:
  2.1 28.8 %collective-permute-start = (bf16[8,8,3072]{2,1,0:T(8,128)(2,1)S(1)}, bf16[8,8,3072]{2,1,0:T(8,128)(2,1)S(1)}, u32[]{:S(2)}, u32[]{:S(2)}) collective-permute-start(bf16[8,8,3072]{2,1,0:T(8,128)(2,1)S(1)} %get-tuple-element.407), channel_id=1, source_target_pairs={{0,16},{16,32},{32,48},{48,64},{64,80},{80,96},{96,112},{112,128},... | collective-permute-start | bytes 1179656 | tf_op jit(solution)/shard_map/ppermute | solution.py:21
  12.4 18.5 %collective-permute-start.1 = (bf16[8,8,3072]{2,1,0:T(8,128)(2,1)S(1)}, bf16[8,8,3072]{2,1,0:T(8,128)(2,1)S(1)}, u32[]{:S(2)}, u32[]{:S(2)}) collective-permute-start(bf16[8,8,3072]{2,1,0:T(8,128)(2,1)S(1)} %get-tuple-element.408), channel_id=1, source_target_pairs={{16,0},{32,16},{48,32},{64,48},{80,64},{96,80},{112,96},{128,112},... | collective-permute-start | bytes 1179656 | tf_op jit(solution)/shard_map/ppermute | solution.py:24
  32.4 77.4 %collective-permute-start.2 = (bf16[32,8,3072]{2,1,0:T(8,128)(2,1)}, bf16[32,8,3072]{2,1,0:T(8,128)(2,1)}, u32[]{:S(2)}, u32[]{:S(2)}) collective-permute-start(bf16[32,8,3072]{2,1,0:T(8,128)(2,1)} %pad_maximum_fusion.2), channel_id=1, source_target_pairs={{0,1},{1,2},{2,3},{3,4},{4,5},{5,6},{6,7},{7,8},{8,9},{9,10},{10,1... | collective-permute-start | bytes 4718600 | tf_op jit(solution)/shard_map/ppermute | solution.py:21
  35.5 74.3 %collective-permute-start.3 = (bf16[32,8,3072]{2,1,0:T(8,128)(2,1)}, bf16[32,8,3072]{2,1,0:T(8,128)(2,1)}, u32[]{:S(2)}, u32[]{:S(2)}) collective-permute-start(bf16[32,8,3072]{2,1,0:T(8,128)(2,1)} %pad_maximum_fusion.2), channel_id=1, source_target_pairs={{1,0},{2,1},{3,2},{4,3},{5,4},{6,5},{7,6},{8,7},{9,8},{10,9},{11,1... | collective-permute-start | bytes 4718600 | tf_op jit(solution)/shard_map/ppermute | solution.py:24
  41.8 52.9 %collective-permute-start.4 = (bf16[8,8,3072]{2,1,0:T(8,128)(2,1)}, bf16[8,8,3072]{2,1,0:T(8,128)(2,1)S(1)}, u32[]{:S(2)}, u32[]{:S(2)}) collective-permute-start(bf16[8,8,3072]{2,1,0:T(8,128)(2,1)} %get-tuple-element.409), channel_id=1, source_target_pairs={{0,16},{16,32},{32,48},{48,64},{64,80},{80,96},{96,112},{112,128},... | collective-permute-start | bytes 1179656 | tf_op jit(solution)/shard_map/ppermute | solution.py:21
  50.7 50.4 %collective-permute-start.5 = (bf16[8,8,3072]{2,1,0:T(8,128)(2,1)}, bf16[8,8,3072]{2,1,0:T(8,128)(2,1)S(1)}, u32[]{:S(2)}, u32[]{:S(2)}) collective-permute-start(bf16[8,8,3072]{2,1,0:T(8,128)(2,1)} %get-tuple-element.410), channel_id=1, source_target_pairs={{16,0},{32,16},{48,32},{64,48},{80,64},{96,80},{112,96},{128,112},... | collective-permute-start | bytes 1179656 | tf_op jit(solution)/shard_map/ppermute | solution.py:24
  94.6 19.9 %copy-start.2 = (bf16[8,8,3072]{2,1,0:T(8,128)(2,1)}, bf16[8,8,3072]{2,1,0:T(8,128)(2,1)S(1)}, u32[]{:S(2)}) copy-start(bf16[8,8,3072]{2,1,0:T(8,128)(2,1)S(1)} %collective-permute-done.4) | copy-start | bytes 1179652
  101.1 13.5 %copy-start.3 = (bf16[8,8,3072]{2,1,0:T(8,128)(2,1)}, bf16[8,8,3072]{2,1,0:T(8,128)(2,1)S(1)}, u32[]{:S(2)}) copy-start(bf16[8,8,3072]{2,1,0:T(8,128)(2,1)S(1)} %collective-permute-done.5) | copy-start | bytes 1179652
  102.4 92.1 %collective-permute-start.6 = (bf16[32,8,3072]{2,1,0:T(8,128)(2,1)}, bf16[32,8,3072]{2,1,0:T(8,128)(2,1)}, u32[]{:S(2)}, u32[]{:S(2)}) collective-permute-start(bf16[32,8,3072]{2,1,0:T(8,128)(2,1)} %pad_maximum_fusion.3), channel_id=1, source_target_pairs={{0,1},{1,2},{2,3},{3,4},{4,5},{5,6},{6,7},{7,8},{8,9},{9,10},{10,1... | collective-permute-start | bytes 4718600 | tf_op jit(solution)/shard_map/ppermute | solution.py:21
  104.4 90.2 %collective-permute-start.7 = (bf16[32,8,3072]{2,1,0:T(8,128)(2,1)}, bf16[32,8,3072]{2,1,0:T(8,128)(2,1)}, u32[]{:S(2)}, u32[]{:S(2)}) collective-permute-start(bf16[32,8,3072]{2,1,0:T(8,128)(2,1)} %pad_maximum_fusion.3), channel_id=1, source_target_pairs={{1,0},{2,1},{3,2},{4,3},{5,4},{6,5},{7,6},{8,7},{9,8},{10,9},{11,1... | collective-permute-start | bytes 4718600 | tf_op jit(solution)/shard_map/ppermute | solution.py:24
  174.3 4.7 %collective-permute-start.8 = (f32[8,8,24]{0,2,1:T(8,128)S(1)}, f32[8,8,24]{0,2,1:T(8,128)S(1)}, u32[]{:S(2)}, u32[]{:S(2)}) collective-permute-start(f32[8,8,24]{0,2,1:T(8,128)S(1)} %get-tuple-element.411), channel_id=1, source_target_pairs={{0,16},{16,32},{32,48},{48,64},{64,80},{80,96},{96,112},{112,128},... | collective-permute-start | bytes 18440 | tf_op jit(solution)/shard_map/ppermute | solution.py:21
  177.0 9.8 %collective-permute-start.9 = (f32[8,8,24]{0,2,1:T(8,128)S(1)}, f32[8,8,24]{0,2,1:T(8,128)S(1)}, u32[]{:S(2)}, u32[]{:S(2)}) collective-permute-start(f32[8,8,24]{0,2,1:T(8,128)S(1)} %get-tuple-element.412), channel_id=1, source_target_pairs={{16,0},{32,16},{48,32},{64,48},{80,64},{96,80},{112,96},{128,112},... | collective-permute-start | bytes 18440 | tf_op jit(solution)/shard_map/ppermute | solution.py:24
  187.0 12.7 %collective-permute-start.10 = (f32[32,8,24]{0,2,1:T(8,128)S(1)}, f32[32,8,24]{0,2,1:T(8,128)S(1)}, u32[]{:S(2)}, u32[]{:S(2)}) collective-permute-start(f32[32,8,24]{0,2,1:T(8,128)S(1)} %pad_maximum_fusion.6), channel_id=1, source_target_pairs={{0,1},{1,2},{2,3},{3,4},{4,5},{5,6},{6,7},{7,8},{8,9},{9,10},{10,1... | collective-permute-start | bytes 73736 | tf_op jit(solution)/shard_map/ppermute | solution.py:21
  188.9 10.8 %collective-permute-start.11 = (f32[32,8,24]{0,2,1:T(8,128)S(1)}, f32[32,8,24]{0,2,1:T(8,128)S(1)}, u32[]{:S(2)}, u32[]{:S(2)}) collective-permute-start(f32[32,8,24]{0,2,1:T(8,128)S(1)} %pad_maximum_fusion.6), channel_id=1, source_target_pairs={{1,0},{2,1},{3,2},{4,3},{5,4},{6,5},{7,6},{8,7},{9,8},{10,9},{11,1... | collective-permute-start | bytes 73736 | tf_op jit(solution)/shard_map/ppermute | solution.py:24
  211.4 3.1 %copy-start = (bf16[576,12,128]{2,1,0:T(8,128)(2,1)S(1)}, bf16[576,12,128]{2,1,0:T(8,128)(2,1)}, u32[]{:S(2)}) copy-start(bf16[576,12,128]{2,1,0:T(8,128)(2,1)} %reshape.463) | copy-start | bytes 5308420 | tf_op jit(solution)/shard_map/while
  217.1 3.1 %copy-start.1 = (bf16[16,8,1536]{2,1,0:T(8,128)(2,1)S(1)}, bf16[16,8,1536]{2,1,0:T(8,128)(2,1)}, u32[]{:S(2)}) copy-start(bf16[16,8,1536]{2,1,0:T(8,128)(2,1)} %get-tuple-element.667) | copy-start | bytes 1179652 | tf_op jit(solution)/shard_map/while
  238.4 3.1 %copy-start = (bf16[576,12,128]{2,1,0:T(8,128)(2,1)S(1)}, bf16[576,12,128]{2,1,0:T(8,128)(2,1)}, u32[]{:S(2)}) copy-start(bf16[576,12,128]{2,1,0:T(8,128)(2,1)} %reshape.463) | copy-start | bytes 5308420 | tf_op jit(solution)/shard_map/while
  244.1 3.1 %copy-start.1 = (bf16[16,8,1536]{2,1,0:T(8,128)(2,1)S(1)}, bf16[16,8,1536]{2,1,0:T(8,128)(2,1)}, u32[]{:S(2)}) copy-start(bf16[16,8,1536]{2,1,0:T(8,128)(2,1)} %get-tuple-element.667) | copy-start | bytes 1179652 | tf_op jit(solution)/shard_map/while
where the time goes:
time: 259 us; the launch traced here: 258 us
  waiting for transfers between devices  71.8 us (28%)
  local copies, waits for them, and re-layouts  61.7 us (24%)
  starting transfers between devices  50 us (19%)
  matrix products  39.4 us (15%)
  other arithmetic  17.9 us (7%)
  loops' own time  16.5 us (6%)
    ppermute x6, waiting for transfers between devices, padded(): lax.ppermute(lax.slice_in_dim(block, block.shape[dim] - width, None, axis...  57.6 us
    ppermute x6, starting transfers between devices, padded(): lax.ppermute(lax.slice_in_dim(block, block.shape[dim] - width, None, axis...  28.8 us
    reshape x16, local copies, waits for them, and re-layouts, split_heads(): return block.reshape(-1, block.shape[-1] // HEAD_DIM, HEAD_DIM)  26.4 us
    ppermute x6, starting transfers between devices, padded(): lax.ppermute(lax.slice_in_dim(block, 0, width, axis=dim), axis, backward)  21.2 us
    ppermute x6, waiting for transfers between devices, padded(): lax.ppermute(lax.slice_in_dim(block, 0, width, axis=dim), axis, backward)  14.3 us
    concatenate x6, other arithmetic, padded(): block = jnp.concatenate([low, block, high], axis=dim)  12.8 us
    another operation x1, loops' own time, per_device(): key_bands, value_bands = lax.map(key_step, starts)  8.61 us
    dot_general x2, matrix products, query_terms(): jnp.einsum('qhd,khd->hqk', grad_heads, value_heads, preferred_element_typ...  8.27 us
  transfers between devices with their start and end apart: 12, of which 4 were waited for; matrix products, arithmetic and copies ran while one was open for 26% of the time, Pallas kernels for 0%

commit v1 on v0

v1 whole, which is shorter than its diff:
```python
import functools
import math

import jax
import jax.numpy as jnp
from jax import lax
from jax.experimental import pallas as pl
from jax.experimental.pallas import tpu as pltpu
from jax.sharding import PartitionSpec as P

HEAD_DIM = 128
RADIUS = 8
TILE_ROWS = 16
TILE_COLS = 8
TOKENS = TILE_ROWS * TILE_COLS
CELL = 64
BLOCK = 2 * TOKENS
WINDOW = 3 * BLOCK
FLOOR = -1e30
MESH = pl.DeviceIdType.MESH
LOOK = 2

OUT, SIB, LEFT, RIGHT, OUT_LEFT, OUT_RIGHT, SIB_LEFT, SIB_RIGHT = range(8)


def dot(a, b, dims):
    return lax.dot_general(a, b, (dims, ((), ())), preferred_element_type=jnp.float32)


def fill_bias(bias, row, col, grid_rows, grid_cols):
    own = lax.broadcasted_iota(jnp.int32, (TOKENS, TOKENS), 0)
    lane = lax.broadcasted_iota(jnp.int32, (TOKENS, TOKENS), 1)
    own_row, own_col = own >> 3, own & 7
    for block in range(3):
        for half in range(2):
            if half == 0:
                key_row = lane >> 3
            else:
                key_row = jnp.where(lane < CELL, 16 + (lane >> 3), (lane >> 3) - 16)
            key_col = (lane & 7) + (block - 1) * TILE_COLS
            grid_row = key_row + row * TILE_ROWS
            grid_col = key_col + col * TILE_COLS
            ok = (
                (jnp.abs(own_row - key_row) <= RADIUS)
                & (jnp.abs(own_col - key_col) <= RADIUS)
                & (grid_row >= 0)
                & (grid_row < grid_rows)
                & (grid_col >= 0)
                & (grid_col < grid_cols)
            )
            start = block * BLOCK + half * TOKENS
            bias[:, start : start + TOKENS] = jnp.where(ok, 0.0, FLOOR)


def kernel(
    heads, rows, cols,
    q_ref, k_ref, v_ref, g_ref, out_ref,
    win, bias, stat_out, stat_in, load_sem, send_sem, recv_sem, stat_send, stat_recv,
):
    row, col = lax.axis_index("row"), lax.axis_index("col")
    core = lax.rem(row, 2)
    outside = row - 1 + 2 * core
    sibling = row + 1 - 2 * core
    has_out = (outside >= 0) & (outside < rows)
    has_left = col > 0
    has_right = col < cols - 1
    has_up = row > 0
    has_down = row < rows - 1
    around = []
    for dr in (-1, 0, 1):
        for dc in (-1, 0, 1):
            if dr == 0 and dc == 0:
                continue
            there = None
            for cond in ([has_up, None, has_down][dr + 1], [has_left, None, has_right][dc + 1]):
                if cond is not None:
                    there = cond if there is None else there & cond
            around.append((dr, dc, there))

    loads = []
    for a, ref in enumerate((q_ref, k_ref, v_ref, g_ref)):
        copy = pltpu.make_async_copy(ref, win.at[a, pl.ds(BLOCK, TOKENS)], load_sem.at[a])
        copy.start()
        loads.append(copy)

    barrier = pltpu.get_barrier_semaphore()
    for dr, dc, there in around:
        @pl.when(there)
        def _():
            pl.semaphore_signal(barrier, inc=1, device_id=(row + dr, col + dc), device_id_type=MESH)
    n_rows = 1 + has_up.astype(jnp.int32) + has_down.astype(jnp.int32)
    n_cols = 1 + has_left.astype(jnp.int32) + has_right.astype(jnp.int32)
    pl.semaphore_wait(barrier, n_rows * n_cols - 1)
    for copy in loads:
        copy.wait()

    far = 1 - core
    out_slot = pl.multiple_of(TOKENS + far * CELL, CELL)
    sib_slot = pl.multiple_of(TOKENS + core * CELL, CELL)

    def lanes(k):
        return pl.ds(pl.multiple_of(k * HEAD_DIM, HEAD_DIM), HEAD_DIM)

    whole = pl.ds(0, heads * HEAD_DIM)

    def move(kind, k, channels, src_start, dst_start, count, peer):
        return pltpu.make_async_remote_copy(
            src_ref=win.at[:, pl.ds(src_start, count), channels],
            dst_ref=win.at[:, pl.ds(dst_start, count), channels],
            send_sem=send_sem.at[kind],
            recv_sem=recv_sem.at[kind, k],
            device_id=peer,
            device_id_type=MESH,
        )

    def flow(kind, k, channels):
        at = pl.multiple_of
        if kind == OUT:
            return move(kind, k, channels, at(BLOCK + core * CELL, CELL),
                        at(BLOCK + TOKENS + core * CELL, CELL), CELL, (outside, col))
        if kind == SIB:
            return move(kind, k, channels, at(BLOCK + far * CELL, CELL),
                        at(BLOCK + TOKENS + far * CELL, CELL), CELL, (sibling, col))
        if kind == LEFT:
            return move(kind, k, channels, BLOCK, 0, TOKENS, (row, col + 1))
        if kind == RIGHT:
            return move(kind, k, channels, BLOCK, 2 * BLOCK, TOKENS, (row, col - 1))
        if kind == OUT_LEFT:
            return move(kind, k, channels, at(BLOCK + out_slot, CELL), out_slot, CELL, (row, col + 1))
        if kind == OUT_RIGHT:
            return move(kind, k, channels, at(BLOCK + out_slot, CELL), at(2 * BLOCK + out_slot, CELL), CELL, (row, col - 1))
        if kind == SIB_LEFT:
            return move(kind, k, channels, at(far * CELL, CELL), at(TOKENS + far * CELL, CELL), CELL, (sibling, col))
        return move(kind, k, channels, at(2 * BLOCK + far * CELL, CELL),
                    at(2 * BLOCK + TOKENS + far * CELL, CELL), CELL, (sibling, col))

    sends_if = {
        OUT: has_out, SIB: None, LEFT: has_right, RIGHT: has_left,
        OUT_LEFT: has_out & has_right, OUT_RIGHT: has_out & has_left,
        SIB_LEFT: has_left, SIB_RIGHT: has_right,
    }
    gets_if = {
        OUT: has_out, SIB: None, LEFT: has_left, RIGHT: has_right,
        OUT_LEFT: has_out & has_left, OUT_RIGHT: has_out & has_right,
        SIB_LEFT: has_left, SIB_RIGHT: has_right,
    }

    def when(cond, action):
        if cond is None:
            action()
        else:
            pl.when(cond)(action)

    def send(kind, k):
        when(sends_if[kind], lambda: flow(kind, k, lanes(k)).start())

    def get(kind, k):
        when(gets_if[kind], lambda: flow(kind, k, lanes(k)).wait_recv())

    @pl.loop(0, heads)
    def _(k):
        for kind in (OUT, LEFT, RIGHT, SIB):
            send(kind, k)

    def clear(start, count):
        win[:, pl.ds(start, count), :] = jnp.zeros((4, count, heads * HEAD_DIM), win.dtype)

    @pl.when(jnp.logical_not(has_left))
    def _():
        clear(0, BLOCK)

    @pl.when(jnp.logical_not(has_right))
    def _():
        clear(2 * BLOCK, BLOCK)

    @pl.when(jnp.logical_not(has_out))
    def _():
        for block in range(3):
            clear(pl.multiple_of(block * BLOCK + out_slot, CELL), CELL)

    for dr, dc, there in around:
        slot = (dr + 1) * 3 + dc + 1

        @pl.when(jnp.logical_not(there))
        def _():
            stat_in[slot] = jnp.zeros(stat_in.shape[1:], stat_in.dtype)

    fill_bias(bias, row, col, rows * TILE_ROWS, cols * TILE_COLS)

    scale = 1.0 / math.sqrt(HEAD_DIM)
    scale2 = scale / math.log(2.0)
    own = pl.ds(BLOCK, TOKENS)

    def stat_move(index, k, src, dst):
        dr, dc, _ = around[index]
        return pltpu.make_async_remote_copy(
            src_ref=src, dst_ref=dst,
            send_sem=stat_send.at[index], recv_sem=stat_recv.at[index, k],
            device_id=(row + dr, col + dc), device_id_type=MESH,
        )

    def forward(k):
        get(OUT, k)
        send(OUT_LEFT, k)
        send(OUT_RIGHT, k)
        get(LEFT, k)
        send(SIB_LEFT, k)
        get(RIGHT, k)
        send(SIB_RIGHT, k)

    def query_pass(k):
        for kind in (SIB, OUT_LEFT, OUT_RIGHT, SIB_LEFT, SIB_RIGHT):
            get(kind, k)
        channels = lanes(k)
        keys = win[1, :, channels]
        scores = dot(win[0, own, channels], keys, ((1,), (1,))) * scale2 + bias[...]
        peak = jnp.max(scores, axis=1, keepdims=True)
        weights = jnp.exp2(scores - peak)
        total = jnp.sum(weights, axis=1, keepdims=True)
        grad_prob = dot(win[3, own, channels], win[2, :, channels], ((1,), (1,)))
        inverse = 1.0 / total
        offset = jnp.sum(weights * grad_prob, axis=1, keepdims=True) * inverse
        grad_score = ((weights * inverse) * (grad_prob - offset)).astype(jnp.bfloat16)
        out_ref[:, channels] = (dot(grad_score, keys, ((1,), (0,))) * scale).astype(jnp.bfloat16)
        log_total = peak + jnp.log2(total)
        lane = lax.broadcasted_iota(jnp.int32, (TOKENS, TOKENS), 1)
        stats = jnp.where(lane == 0, log_total, jnp.where(lane == 1, offset, 0.0)).T[:8]
        stat_out[k] = stats
        stat_in[4, k] = stats
        for index, (dr, dc, there) in enumerate(around):
            slot = (1 - dr) * 3 + 1 - dc
            when(there, lambda: stat_move(index, k, stat_out.at[k], stat_in.at[slot, k]).start())

    def key_pass(k):
        for index, (dr, dc, there) in enumerate(around):
            when(there, lambda: stat_move(7 - index, k, stat_out.at[k], stat_in.at[(dr + 1) * 3 + dc + 1, k]).wait_recv())
        channels = lanes(k)
        lane = lax.broadcasted_iota(jnp.int32, (1, TOKENS), 1)
        totals, offsets = [], []
        for block in range(3):
            for which, parts in ((0, totals), (1, offsets)):
                parts.append(stat_in[3 + block, k, which : which + 1, :])
                parts.append(
                    jnp.where(
                        lane < CELL,
                        stat_in[6 + block, k, which : which + 1, :],
                        stat_in[block, k, which : which + 1, :],
                    )
                )
        log_total = jnp.concatenate(totals, axis=1)
        offset = jnp.concatenate(offsets, axis=1)
        queries, grads = win[0, :, channels], win[3, :, channels]
        scores = dot(win[1, own, channels], queries, ((1,), (1,))) * scale2 + bias[...]
        weights = jnp.exp2(scores - log_total)
        grad_prob = dot(win[2, own, channels], grads, ((1,), (1,)))
        grad_score = (weights * (grad_prob - offset)).astype(jnp.bfloat16)
        key_lanes = pl.ds(pl.multiple_of((heads + k) * HEAD_DIM, HEAD_DIM), HEAD_DIM)
        value_lanes = pl.ds(pl.multiple_of((2 * heads + k) * HEAD_DIM, HEAD_DIM), HEAD_DIM)
        out_ref[:, key_lanes] = (dot(grad_score, queries, ((1,), (0,))) * scale).astype(jnp.bfloat16)
        out_ref[:, value_lanes] = dot(weights.astype(jnp.bfloat16), grads, ((1,), (0,))).astype(jnp.bfloat16)

    look = min(LOOK, heads)

    @pl.loop(0, look)
    def _(k):
        forward(k)

    @pl.loop(0, heads)
    def _(k):
        @pl.when(k + look < heads)
        def _():
            forward(k + look)

        query_pass(k)

        @pl.when(k > 0)
        def _():
            key_pass(k - 1)

    key_pass(heads - 1)

    for kind in range(8):
        when(sends_if[kind], lambda: flow(kind, 0, whole).wait_send())
    for index, (dr, dc, there) in enumerate(around):
        when(there, lambda: stat_move(index, 0, stat_out, stat_in.at[0]).wait_send())


def per_device(queries, keys, values, out_grad):
    tile_rows, tile_cols, channels = queries.shape
    heads = channels // HEAD_DIM
    rows, cols = lax.axis_size("row"), lax.axis_size("col")
    flat = [x.reshape(TOKENS, channels) for x in (queries, keys, values, out_grad)]
    out = pl.pallas_call(
        functools.partial(kernel, heads, rows, cols),
        out_shape=jax.ShapeDtypeStruct((TOKENS, 3 * channels), jnp.bfloat16),
        in_specs=[pl.BlockSpec(memory_space=pl.ANY)] * 4,
        out_specs=pl.BlockSpec(memory_space=pltpu.VMEM),
        scratch_shapes=[
            pltpu.VMEM((4, WINDOW, channels), jnp.bfloat16),
            pltpu.VMEM((TOKENS, WINDOW), jnp.float32),
            pltpu.VMEM((heads, 8, TOKENS), jnp.float32),
            pltpu.VMEM((9, heads, 8, TOKENS), jnp.float32),
            pltpu.SemaphoreType.DMA((4,)),
            pltpu.SemaphoreType.DMA((8,)),
            pltpu.SemaphoreType.DMA((8, heads)),
            pltpu.SemaphoreType.DMA((8,)),
            pltpu.SemaphoreType.DMA((8, heads)),
        ],
        compiler_params=pltpu.CompilerParams(
            collective_id=0, has_side_effects=True, vmem_limit_bytes=40 * 1024 * 1024
        ),
        name="window_backward",
    )(*flat)
    return out.reshape(tile_rows, tile_cols, 3 * channels)


def solution(mesh):
    spec = P("row", "col", None)
    return jax.shard_map(
        per_device, mesh=mesh, in_specs=(spec,) * 4, out_specs=spec, check_vma=False
    )
```

time: 259 us -> 134 us (0.52)
  the two profiles are of different devices: /device:TPU:113 before, /device:TPU:35 now
where the time goes in v1:
time: 134 us
  Pallas kernels  129 us (96%)
  local copies, waits for them, and re-layouts  5 us (4%)
    pallas_call x1, Pallas kernels, per_device(): pl.pallas_call(functools.partial(kernel, heads, rows, cols), out_shape=ja...  129 us
    unnamed x9, local copies, waits for them, and re-layouts  5 us

profile of v1, /device:TPU:35, one launch (start us, length us, event | category | flops | bytes accessed | tf_op | source)
XLA Modules:
  0.0 134.1 jit_solution(14601733899225001375)
XLA Ops:
  0.0 0.0 copy-start
  0.0 1.0 copy-done
  1.0 0.0 copy-start.1
  1.0 1.0 copy-done.1
  2.0 0.0 copy-start.2
  2.0 1.0 copy-done.2
  3.0 0.0 copy-start.3
  3.0 1.0 copy-done.3
  4.0 129.1 %window_backward.1 = bf16[128,4608]{1,0:T(8,128)(2,1)S(1)} custom-call(bf16[128,1536]{1,0:T(8,128)(2,1)S(1)} %bitcast.6, bf16[128,1536]{1,0:T(8,128)(2,1)S(1)} %bitcast.7, bf16[128,1536]{1,0:T(8,128)(2,1)S(1)} %bitcast.8, bf16[128,1536]{1,0:T(8,128)(2,1)S(1)} %bitcast.9), custom_call_target="tpu_custom_call" | custom-call | tf_op jit(solution)/shard_map/window_backward/pallas_call | solution.py:293
  133.1 1.0 copy.6
Async XLA Ops:
  0.0 1.0 copy-start
  1.0 1.0 copy-start.1
  2.0 1.0 copy-start.2
  3.0 1.0 copy-start.3

commit v2 on v1

v2 whole, which is shorter than its diff:
```python
import functools
import math

import jax
import jax.numpy as jnp
from jax import lax
from jax.experimental import pallas as pl
from jax.experimental.pallas import tpu as pltpu
from jax.sharding import PartitionSpec as P

HEAD_DIM = 128
RADIUS = 8
TILE_ROWS = 16
TILE_COLS = 8
TOKENS = TILE_ROWS * TILE_COLS
CELL = 64
BLOCK = 2 * TOKENS
SPAN = 3 * BLOCK
GROUP = 4
BLOCKS = GROUP + 2
FLOOR = -1e30
MESH = pl.DeviceIdType.MESH


def dot(a, b, dims):
    return lax.dot_general(a, b, (dims, ((), ())), preferred_element_type=jnp.float32)


def fill_bias(bias, row, group, grid_rows, grid_cols):
    own = lax.broadcasted_iota(jnp.int32, (TOKENS, TOKENS), 0)
    lane = lax.broadcasted_iota(jnp.int32, (TOKENS, TOKENS), 1)
    own_row, own_col = own >> 3, own & 7

    @pl.loop(0, GROUP)
    def _(tile):
        for block in range(3):
            for half in range(2):
                if half == 0:
                    key_row = lane >> 3
                else:
                    key_row = jnp.where(lane < CELL, 16 + (lane >> 3), (lane >> 3) - 16)
                key_col = (lane & 7) + (block - 1) * TILE_COLS
                grid_row = key_row + row * TILE_ROWS
                grid_col = key_col + (group * GROUP + tile) * TILE_COLS
                ok = (
                    (jnp.abs(own_row - key_row) <= RADIUS)
                    & (jnp.abs(own_col - key_col) <= RADIUS)
                    & (grid_row >= 0)
                    & (grid_row < grid_rows)
                    & (grid_col >= 0)
                    & (grid_col < grid_cols)
                )
                start = block * BLOCK + half * TOKENS
                bias[tile, :, start : start + TOKENS] = jnp.where(ok, 0.0, FLOOR)


def both(*conditions):
    there = None
    for cond in conditions:
        if cond is not None:
            there = cond if there is None else there & cond
    return there


def when(cond, action):
    if cond is None:
        action()
    else:
        pl.when(cond)(action)


def kernel(
    heads, rows, cols,
    q_ref, k_ref, v_ref, g_ref, out_ref,
    mine, win, bias, stats, parts,
    load_sem, local_sem, share_send, share_recv, out_send, out_recv, col_send, col_recv,
    sib_send, sib_recv, stat_send, stat_recv, part_send, part_recv, part_local,
):
    per = heads // GROUP
    row, col = lax.axis_index("row"), lax.axis_index("col")
    core = lax.rem(row, 2)
    x = lax.rem(col, GROUP)
    group = col // GROUP
    first = group * GROUP
    outside = row - 1 + 2 * core
    sibling = row + 1 - 2 * core
    has_out = (outside >= 0) & (outside < rows)
    has_left = group > 0
    has_right = group < cols // GROUP - 1
    has_up = row > 0
    has_down = row < rows - 1
    has_row = {-1: has_up, 0: None, 1: has_down}

    loads = []
    for a, ref in enumerate((q_ref, k_ref, v_ref, g_ref)):
        copy = pltpu.make_async_copy(ref, mine.at[a], load_sem.at[a])
        copy.start()
        loads.append(copy)

    barrier = pltpu.get_barrier_semaphore()

    def greet(device):
        pl.semaphore_signal(barrier, inc=1, device_id=device, device_id_type=MESH)

    for step in range(1, GROUP):
        greet((row, first + lax.rem(x + step, GROUP)))
    greet((sibling, col))

    @pl.when(has_out)
    def _():
        for peer in range(GROUP):
            greet((outside, first + peer))

    for there, shift in ((has_left, -GROUP), (has_right, GROUP)):
        for dr in (-1, 0, 1):
            when(both(there, has_row[dr]), lambda: greet((row + dr, col + shift)))
    sides = has_left.astype(jnp.int32) + has_right.astype(jnp.int32)
    lines = 1 + has_up.astype(jnp.int32) + has_down.astype(jnp.int32)
    pl.semaphore_wait(barrier, GROUP + GROUP * has_out.astype(jnp.int32) + sides * lines)
    for copy in loads:
        copy.wait()

    far = 1 - core
    out_slot = pl.multiple_of(TOKENS + far * CELL, CELL)
    own_rows = pl.ds(0, TOKENS)
    width = per * HEAD_DIM

    def lanes(k):
        if isinstance(k, int):
            return pl.ds(k * HEAD_DIM, HEAD_DIM)
        return pl.ds(pl.multiple_of(k * HEAD_DIM, HEAD_DIM), HEAD_DIM)

    def remote(src, dst, send_sem, recv_sem, device):
        return pltpu.make_async_remote_copy(
            src_ref=src, dst_ref=dst, send_sem=send_sem, recv_sem=recv_sem,
            device_id=device, device_id_type=MESH,
        )

    def share(step, h):
        peer = lax.rem(x + step, GROUP)
        return remote(
            mine.at[:, :, lanes(per * peer + h)], win.at[:, x + 1, own_rows, lanes(h)],
            share_send.at[step], share_recv.at[step, h], (row, first + peer),
        )

    def keep(h):
        return pltpu.make_async_copy(
            mine.at[:, :, lanes(per * x + h)], win.at[:, x + 1, own_rows, lanes(h)], local_sem.at[h]
        )

    def outer(step, h):
        peer = lax.rem(x + step, GROUP)
        return remote(
            mine.at[:, pl.ds(pl.multiple_of(core * CELL, CELL), CELL), lanes(per * peer + h)],
            win.at[:, x + 1, pl.ds(pl.multiple_of(TOKENS + core * CELL, CELL), CELL), lanes(h)],
            out_send.at[step], out_recv.at[step, h], (outside, first + peer),
        )

    def column(kind, h):
        src, dst, shift = ((1, BLOCKS - 1, -GROUP), (GROUP, 0, GROUP))[kind % 2]
        piece = own_rows if kind < 2 else pl.ds(out_slot, CELL)
        return remote(
            win.at[:, src, piece, lanes(h)], win.at[:, dst, piece, lanes(h)],
            col_send.at[kind], col_recv.at[kind, h], (row, col + shift),
        )

    def beside(kind, h):
        start, count = ((1, GROUP), (0, 1), (BLOCKS - 1, 1))[kind]
        return remote(
            win.at[:, pl.ds(start, count), pl.ds(pl.multiple_of(far * CELL, CELL), CELL), lanes(h)],
            win.at[:, pl.ds(start, count), pl.ds(pl.multiple_of(TOKENS + far * CELL, CELL), CELL), lanes(h)],
            sib_send.at[kind], sib_recv.at[kind, h], (sibling, col),
        )

    notices = []
    for dr in (-1, 1):
        notices.append((dr, (1, GROUP), (1, GROUP), 0, has_row[dr], has_row[-dr]))
    for dr in (-1, 0, 1):
        notices.append((dr, (1, 1), (BLOCKS - 1, 1), -GROUP, both(has_left, has_row[dr]), both(has_right, has_row[-dr])))
        notices.append((dr, (GROUP, 1), (0, 1), GROUP, both(has_right, has_row[dr]), both(has_left, has_row[-dr])))

    def notice(index, h):
        dr, src, dst, shift, _, _ = notices[index]
        return remote(
            stats.at[1, h, pl.ds(*src)], stats.at[1 - dr, h, pl.ds(*dst)],
            stat_send.at[index], stat_recv.at[index, h], (row + dr, col + shift),
        )

    def start_share(h):
        keep(h).start()
        for step in range(1, GROUP):
            share(step, h).start()

    def start_outer(h):
        @pl.when(has_out)
        def _():
            for step in range(GROUP):
                outer(step, h).start()

    def spread_own(h):
        for step in range(1, GROUP):
            share(step, h).wait_recv()
        keep(h).wait()
        when(has_left, lambda: column(0, h).start())
        when(has_right, lambda: column(1, h).start())
        beside(0, h).start()

    def spread_outer(h):
        @pl.when(has_out)
        def _():
            for step in range(GROUP):
                outer(step, h).wait_recv()
            when(has_left, lambda: column(2, h).start())
            when(has_right, lambda: column(3, h).start())

    def complete(h):
        @pl.when(has_right)
        def _():
            column(0, h).wait_recv()
            beside(2, h).start()

        @pl.when(has_left)
        def _():
            column(1, h).wait_recv()
            beside(1, h).start()

        beside(0, h).wait_recv()
        when(both(has_right, has_out), lambda: column(2, h).wait_recv())
        when(both(has_left, has_out), lambda: column(3, h).wait_recv())
        when(has_right, lambda: beside(2, h).wait_recv())
        when(has_left, lambda: beside(1, h).wait_recv())

    start_outer(0)
    start_share(0)
    if per > 1:
        start_share(1)

    def clear(block, piece):
        win[:, block, piece, :] = jnp.zeros((4, piece.size, width), win.dtype)

    for there, block in ((has_left, 0), (has_right, BLOCKS - 1)):
        @pl.when(jnp.logical_not(there))
        def _():
            clear(block, pl.ds(0, BLOCK))
            for line in range(3):
                stats[line, :, block] = jnp.zeros((per, 8, TOKENS), stats.dtype)

    @pl.when(jnp.logical_not(has_out))
    def _():
        for block in range(BLOCKS):
            clear(block, pl.ds(out_slot, CELL))

    for dr in (-1, 1):
        @pl.when(jnp.logical_not(has_row[dr]))
        def _():
            stats[1 + dr] = jnp.zeros((per, BLOCKS, 8, TOKENS), stats.dtype)

    fill_bias(bias, row, group, rows * TILE_ROWS, cols * TILE_COLS)

    scale = 1.0 / math.sqrt(HEAD_DIM)
    scale2 = scale / math.log(2.0)

    def span(a, tile, h):
        return win[a, pl.ds(tile, 3), :, lanes(h)].reshape(SPAN, HEAD_DIM)

    def own(a, tile, h):
        return win[a, tile + 1, own_rows, lanes(h)]

    def deliver(which, tile, h, value):
        here = lanes(which * per + h)
        there = lanes(which * heads + per * x + h)
        parts[tile, :, here] = value.astype(parts.dtype)

        @pl.when(tile == x)
        def _():
            pltpu.make_async_copy(parts.at[tile, :, here], out_ref.at[:, there], part_local.at[0]).start()

        @pl.when(tile != x)
        def _():
            remote(
                parts.at[tile, :, here], out_ref.at[:, there],
                part_send.at[tile], part_recv.at[x], (row, first + tile),
            ).start()

    def query_pass(tile, h):
        keys = span(1, tile, h)
        scores = dot(own(0, tile, h), keys, ((1,), (1,))) * scale2 + bias[tile]
        peak = jnp.max(scores, axis=1, keepdims=True)
        weights = jnp.exp2(scores - peak)
        total = jnp.sum(weights, axis=1, keepdims=True)
        grad_prob = dot(own(3, tile, h), span(2, tile, h), ((1,), (1,)))
        inverse = 1.0 / total
        offset = jnp.sum(weights * grad_prob, axis=1, keepdims=True) * inverse
        grad_score = ((weights * inverse) * (grad_prob - offset)).astype(jnp.bfloat16)
        deliver(0, tile, h, dot(grad_score, keys, ((1,), (0,))) * scale)
        log_total = peak + jnp.log2(total)
        lane = lax.broadcasted_iota(jnp.int32, (TOKENS, TOKENS), 1)
        stats[1, h, tile + 1] = jnp.where(lane == 0, log_total, jnp.where(lane == 1, offset, 0.0)).T[:8]

    def key_pass(tile, h):
        lane = lax.broadcasted_iota(jnp.int32, (1, TOKENS), 1)

        def gather(which):
            pieces = []
            for block in range(3):
                here, above, below = (
                    stats[line, h, tile + block, which : which + 1, :] for line in (1, 0, 2)
                )
                pieces += [here, jnp.where(lane < CELL, below, above)]
            return jnp.concatenate(pieces, axis=1)

        log_total, offset = gather(0), gather(1)
        queries, grads = span(0, tile, h), span(3, tile, h)
        scores = dot(own(1, tile, h), queries, ((1,), (1,))) * scale2 + bias[tile]
        weights = jnp.exp2(scores - log_total)
        deliver(2, tile, h, dot(weights.astype(jnp.bfloat16), grads, ((1,), (0,))))
        grad_prob = dot(own(2, tile, h), grads, ((1,), (1,)))
        grad_score = (weights * (grad_prob - offset)).astype(jnp.bfloat16)
        deliver(1, tile, h, dot(grad_score, queries, ((1,), (0,))) * scale)

    def query_passes(h):
        @pl.loop(0, GROUP)
        def _(tile):
            query_pass(tile, h)

        for index in range(len(notices)):
            when(notices[index][4], lambda: notice(index, h).start())

    def key_passes(h):
        for index in range(len(notices)):
            when(notices[index][5], lambda: notice(index, h).wait_recv())

        @pl.loop(0, GROUP)
        def _(tile):
            key_pass(tile, h)

    spread_own(0)
    if per > 1:
        start_outer(1)
    if per > 2:
        start_share(2)
    spread_outer(0)
    for h in range(per):
        if h + 1 < per:
            spread_own(h + 1)
            if h + 2 < per:
                start_outer(h + 2)
            if h + 3 < per:
                start_share(h + 3)
        complete(h)
        query_passes(h)
        if h > 0:
            key_passes(h - 1)
        if h + 1 < per:
            spread_outer(h + 1)
    key_passes(per - 1)

    for step in range(1, GROUP):
        remote(
            win.at[:, 1, own_rows, :], win.at[:, 1, own_rows, :],
            share_send.at[step], share_recv.at[step, 0], (row, first + lax.rem(x + step, GROUP)),
        ).wait_send()

    def sent(block, piece, sem, recv, device):
        remote(win.at[:, block, piece, :], win.at[:, block, piece, :], sem, recv, device).wait_send()

    @pl.when(has_out)
    def _():
        for step in range(GROUP):
            sent(1, pl.ds(out_slot, CELL), out_send.at[step], out_recv.at[step, 0], (outside, col))

    for kind in range(4):
        side = (has_left, has_right)[kind % 2]
        shift = (-GROUP, GROUP)[kind % 2]
        piece = own_rows if kind < 2 else pl.ds(out_slot, CELL)
        when(
            side if kind < 2 else both(side, has_out),
            lambda: sent(1, piece, col_send.at[kind], col_recv.at[kind, 0], (row, col + shift)),
        )
    for kind, count, there in ((0, GROUP, None), (1, 1, has_left), (2, 1, has_right)):
        piece = win.at[:, pl.ds(0, count), pl.ds(0, CELL), :]
        when(there, lambda: remote(
            piece, piece, sib_send.at[kind], sib_recv.at[kind, 0], (sibling, col)
        ).wait_send())
    for index, (dr, src, _, shift, there, _) in enumerate(notices):
        piece = stats.at[1, :, pl.ds(*src)]
        when(there, lambda: remote(
            piece, piece, stat_send.at[index], stat_recv.at[index, 0], (row + dr, col + shift)
        ).wait_send())
    pltpu.make_async_copy(parts.at[0], parts.at[0], part_local.at[0]).wait()
    for peer in range(GROUP):
        @pl.when(peer != x)
        def _():
            copy = remote(parts.at[peer], parts.at[peer], part_send.at[peer], part_recv.at[peer], (row, first + peer))
            copy.wait_send()
            copy.wait_recv()


def per_device(queries, keys, values, out_grad):
    tile_rows, tile_cols, channels = queries.shape
    heads = channels // HEAD_DIM
    per = heads // GROUP
    rows, cols = lax.axis_size("row"), lax.axis_size("col")
    flat = [x.reshape(TOKENS, channels) for x in (queries, keys, values, out_grad)]
    dma = pltpu.SemaphoreType.DMA
    out = pl.pallas_call(
        functools.partial(kernel, heads, rows, cols),
        out_shape=jax.ShapeDtypeStruct((TOKENS, 3 * channels), jnp.bfloat16),
        in_specs=[pl.BlockSpec(memory_space=pl.ANY)] * 4,
        out_specs=pl.BlockSpec(memory_space=pltpu.VMEM),
        scratch_shapes=[
            pltpu.VMEM((4, TOKENS, channels), jnp.bfloat16),
            pltpu.VMEM((4, BLOCKS, BLOCK, per * HEAD_DIM), jnp.bfloat16),
            pltpu.VMEM((GROUP, TOKENS, SPAN), jnp.float32),
            pltpu.VMEM((3, per, BLOCKS, 8, TOKENS), jnp.float32),
            pltpu.VMEM((GROUP, TOKENS, 3 * per * HEAD_DIM), jnp.bfloat16),
            dma((4,)),
            dma((per,)),
            dma((GROUP,)),
            dma((GROUP, per)),
            dma((GROUP,)),
            dma((GROUP, per)),
            dma((4,)),
            dma((4, per)),
            dma((3,)),
            dma((3, per)),
            dma((8,)),
            dma((8, per)),
            dma((GROUP,)),
            dma((GROUP,)),
            dma((1,)),
        ],
        compiler_params=pltpu.CompilerParams(
            collective_id=0, has_side_effects=True, vmem_limit_bytes=60 * 1024 * 1024
        ),
        name="window_backward",
    )(*flat)
    return out.reshape(tile_rows, tile_cols, 3 * channels)


def solution(mesh):
    spec = P("row", "col", None)
    return jax.shard_map(
        per_device, mesh=mesh, in_specs=(spec,) * 4, out_specs=spec, check_vma=False
    )
```

time: 134 us -> 87.3 us (0.65)
  the two profiles are of different devices: /device:TPU:35 before, /device:TPU:1 now
where the time goes in v2:
time: 87.3 us; the launch traced here: 87.2 us
  Pallas kernels  84.8 us (97%)
  local copies, waits for them, and re-layouts  2.36 us (3%)
    pallas_call x1, Pallas kernels, per_device(): pl.pallas_call(functools.partial(kernel, heads, rows, cols), out_shape=ja...  84.8 us
    unnamed x1, local copies, waits for them, and re-layouts  2.36 us

profile of v2, /device:TPU:1, one launch (start us, length us, event | category | flops | bytes accessed | tf_op | source)
XLA Modules:
  0.0 87.2 jit_solution(5718354573454865711)
XLA Ops:
  0.0 84.8 %window_backward.1 = bf16[128,4608]{1,0:T(8,128)(2,1)} custom-call(bf16[128,1536]{1,0:T(8,128)(2,1)} %bitcast.6, bf16[128,1536]{1,0:T(8,128)(2,1)} %bitcast.7, bf16[128,1536]{1,0:T(8,128)(2,1)} %bitcast.8, bf16[128,1536]{1,0:T(8,128)(2,1)} %bitcast.9), custom_call_target="tpu_custom_call" | custom-call | tf_op jit(solution)/shard_map/window_backward/pallas_call | solution.py:406
  84.8 2.4 %copy.6 = bf16[16,8,4608]{2,1,0:T(8,128)(2,1)} copy(bf16[16,8,4608]{2,1,0:T(8,128)(2,1)} %bitcast.5) | data formatting | bytes 2359296

commit v3 on v2

v3 whole, which is shorter than its diff:
```python
import functools
import math

import jax
import jax.numpy as jnp
from jax import lax
from jax.experimental import pallas as pl
from jax.experimental.pallas import tpu as pltpu
from jax.sharding import PartitionSpec as P

HEAD_DIM = 128
RADIUS = 8
TILE_ROWS = 16
TILE_COLS = 8
TOKENS = TILE_ROWS * TILE_COLS
CELL = 64
BLOCK = 2 * TOKENS
SPAN = 3 * BLOCK
KV = pl.ds(1, 2)
GROUP = 4
BLOCKS = GROUP + 2
FLOOR = -1e30
MESH = pl.DeviceIdType.MESH


def dot(a, b, dims):
    return lax.dot_general(a, b, (dims, ((), ())), preferred_element_type=jnp.float32)


def fill_bias(bias, row, group, grid_rows, grid_cols):
    line = lax.broadcasted_iota(jnp.int32, (TOKENS, TOKENS), 0)
    own = lax.broadcasted_iota(jnp.int32, (TOKENS, TOKENS), 1)
    own_row, own_col = own >> 3, own & 7

    @pl.loop(0, GROUP)
    def _(tile):
        for block in range(3):
            for half in range(2):
                if half == 0:
                    key_row = line >> 3
                else:
                    key_row = jnp.where(line < CELL, 16 + (line >> 3), (line >> 3) - 16)
                key_col = (line & 7) + (block - 1) * TILE_COLS
                grid_row = key_row + row * TILE_ROWS
                grid_col = key_col + (group * GROUP + tile) * TILE_COLS
                ok = (
                    (jnp.abs(own_row - key_row) <= RADIUS)
                    & (jnp.abs(own_col - key_col) <= RADIUS)
                    & (grid_row >= 0)
                    & (grid_row < grid_rows)
                    & (grid_col >= 0)
                    & (grid_col < grid_cols)
                )
                start = block * BLOCK + half * TOKENS
                bias[tile, start : start + TOKENS, :] = jnp.where(ok, 0.0, FLOOR)


def both(*conditions):
    there = None
    for cond in conditions:
        if cond is not None:
            there = cond if there is None else there & cond
    return there


def when(cond, action):
    if cond is None:
        action()
    else:
        pl.when(cond)(action)


def kernel(
    heads, rows, cols,
    q_ref, k_ref, v_ref, g_ref, out_ref,
    mine, win, bias, acc, sib_from, sib_to, col_from, col_to, out_from, out_to, parts,
    load_sem, local_sem, share_send, share_recv, out_send, out_recv, col_send, col_recv,
    sib_send, sib_recv, back_sib_send, back_sib_recv, back_col_send, back_col_recv,
    back_out_send, back_out_recv, part_send, part_recv, part_local,
):
    per = heads // GROUP
    row, col = lax.axis_index("row"), lax.axis_index("col")
    core = lax.rem(row, 2)
    x = lax.rem(col, GROUP)
    group = col // GROUP
    first = group * GROUP
    outside = row - 1 + 2 * core
    sibling = row + 1 - 2 * core
    has_out = (outside >= 0) & (outside < rows)
    has_left = group > 0
    has_right = group < cols // GROUP - 1
    loads = []
    for a, ref in enumerate((q_ref, k_ref, v_ref, g_ref)):
        copy = pltpu.make_async_copy(ref, mine.at[a], load_sem.at[a])
        copy.start()
        loads.append(copy)

    barrier = pltpu.get_barrier_semaphore()

    def greet(device):
        pl.semaphore_signal(barrier, inc=1, device_id=device, device_id_type=MESH)

    for step in range(1, GROUP):
        greet((row, first + lax.rem(x + step, GROUP)))
    greet((sibling, col))

    @pl.when(has_out)
    def _():
        for peer in range(GROUP):
            greet((outside, first + peer))

    for there, shift in ((has_left, -GROUP), (has_right, GROUP)):
        when(there, lambda: greet((row, col + shift)))
    sides = has_left.astype(jnp.int32) + has_right.astype(jnp.int32)
    pl.semaphore_wait(barrier, GROUP + GROUP * has_out.astype(jnp.int32) + sides)
    for copy in loads:
        copy.wait()

    far = 1 - core
    out_slot = pl.multiple_of(TOKENS + far * CELL, CELL)
    own_rows = pl.ds(0, TOKENS)
    width = per * HEAD_DIM

    def lanes(k):
        if isinstance(k, int):
            return pl.ds(k * HEAD_DIM, HEAD_DIM)
        return pl.ds(pl.multiple_of(k * HEAD_DIM, HEAD_DIM), HEAD_DIM)

    def remote(src, dst, send_sem, recv_sem, device):
        return pltpu.make_async_remote_copy(
            src_ref=src, dst_ref=dst, send_sem=send_sem, recv_sem=recv_sem,
            device_id=device, device_id_type=MESH,
        )

    def share(step, h):
        peer = lax.rem(x + step, GROUP)
        return remote(
            mine.at[:, :, lanes(per * peer + h)], win.at[:, x + 1, own_rows, lanes(h)],
            share_send.at[step], share_recv.at[step, h], (row, first + peer),
        )

    def keep(h):
        return pltpu.make_async_copy(
            mine.at[:, :, lanes(per * x + h)], win.at[:, x + 1, own_rows, lanes(h)], local_sem.at[h]
        )

    def outer(step, h):
        peer = lax.rem(x + step, GROUP)
        return remote(
            mine.at[KV, pl.ds(pl.multiple_of(core * CELL, CELL), CELL), lanes(per * peer + h)],
            win.at[KV, x + 1, pl.ds(pl.multiple_of(TOKENS + core * CELL, CELL), CELL), lanes(h)],
            out_send.at[step], out_recv.at[step, h], (outside, first + peer),
        )

    def column(kind, h):
        src, dst, shift = ((1, BLOCKS - 1, -GROUP), (GROUP, 0, GROUP))[kind % 2]
        piece = own_rows if kind < 2 else pl.ds(out_slot, CELL)
        return remote(
            win.at[KV, src, piece, lanes(h)], win.at[KV, dst, piece, lanes(h)],
            col_send.at[kind], col_recv.at[kind, h], (row, col + shift),
        )

    def beside(kind, h):
        start, count = ((1, GROUP), (0, 1), (BLOCKS - 1, 1))[kind]
        return remote(
            win.at[KV, pl.ds(start, count), pl.ds(pl.multiple_of(far * CELL, CELL), CELL), lanes(h)],
            win.at[KV, pl.ds(start, count), pl.ds(pl.multiple_of(TOKENS + far * CELL, CELL), CELL), lanes(h)],
            sib_send.at[kind], sib_recv.at[kind, h], (sibling, col),
        )

    def back_sib(h):
        return remote(sib_from.at[h], sib_to.at[h], back_sib_send.at[0], back_sib_recv.at[h], (sibling, col))

    def back_col(side, h):
        return remote(
            col_from.at[h, side], col_to.at[h, side],
            back_col_send.at[side], back_col_recv.at[side, h], (row, col + (-GROUP, GROUP)[side]),
        )

    def back_out(tile, h):
        return remote(
            out_from.at[h, tile], out_to.at[:, :, lanes(per * x + h)],
            back_out_send.at[tile], back_out_recv.at[x, h], (outside, first + tile),
        )

    def start_share(h):
        keep(h).start()
        for step in range(1, GROUP):
            share(step, h).start()

    def start_outer(h):
        @pl.when(has_out)
        def _():
            for step in range(GROUP):
                outer(step, h).start()

    def spread_own(h):
        for step in range(1, GROUP):
            share(step, h).wait_recv()
        keep(h).wait()
        when(has_left, lambda: column(0, h).start())
        when(has_right, lambda: column(1, h).start())
        beside(0, h).start()

    def spread_outer(h):
        @pl.when(has_out)
        def _():
            for step in range(GROUP):
                outer(step, h).wait_recv()
            when(has_left, lambda: column(2, h).start())
            when(has_right, lambda: column(3, h).start())

    def spread_edges(h):
        @pl.when(has_right)
        def _():
            column(0, h).wait_recv()
            beside(2, h).start()

        @pl.when(has_left)
        def _():
            column(1, h).wait_recv()
            beside(1, h).start()

    def complete_edges(h):
        when(both(has_right, has_out), lambda: column(2, h).wait_recv())
        when(both(has_left, has_out), lambda: column(3, h).wait_recv())
        when(has_right, lambda: beside(2, h).wait_recv())
        when(has_left, lambda: beside(1, h).wait_recv())

    def clear(block, piece):
        win[:, block, piece, :] = jnp.zeros((4, piece.size, width), win.dtype)

    def setup():
        for there, block in ((has_left, 0), (has_right, BLOCKS - 1)):
            @pl.when(jnp.logical_not(there))
            def _():
                clear(block, pl.ds(0, BLOCK))

        @pl.when(jnp.logical_not(has_out))
        def _():
            for block in range(BLOCKS):
                clear(block, pl.ds(out_slot, CELL))

        fill_bias(bias, row, group, rows * TILE_ROWS, cols * TILE_COLS)

        @pl.loop(0, per * 2 * BLOCKS)
        def _(i):
            acc[i // (2 * BLOCKS), lax.rem(i // BLOCKS, 2), lax.rem(i, BLOCKS)] = jnp.zeros(
                (BLOCK, HEAD_DIM), acc.dtype
            )

    scale = 1.0 / math.sqrt(HEAD_DIM)
    scale2 = scale / math.log(2.0)

    def span(a, tile, h):
        return win[a, pl.ds(tile, 3), :, lanes(h)].reshape(SPAN, HEAD_DIM)

    def own(a, tile, h):
        return win[a, tile + 1, own_rows, lanes(h)]

    def deliver(which, tile, h, value):
        here = lanes(which * per + h)
        there = lanes(which * heads + per * x + h)
        parts[tile, :, here] = value.astype(parts.dtype)

        @pl.when(tile == x)
        def _():
            pltpu.make_async_copy(parts.at[tile, :, here], out_ref.at[:, there], part_local.at[0]).start()

        @pl.when(tile != x)
        def _():
            remote(
                parts.at[tile, :, here], out_ref.at[:, there],
                part_send.at[tile], part_recv.at[x], (row, first + tile),
            ).start()

    def tile_pass(tile, h):
        keys = span(1, tile, h)
        queries, grads = own(0, tile, h), own(3, tile, h)
        scores = dot(keys, queries, ((1,), (1,))) * scale2 + bias[tile]
        peak = jnp.max(scores, axis=0, keepdims=True)
        weights = jnp.exp2(scores - peak)
        inverse = 1.0 / jnp.sum(weights, axis=0, keepdims=True)
        grad_prob = dot(span(2, tile, h), grads, ((1,), (1,)))
        offset = jnp.sum(weights * grad_prob, axis=0, keepdims=True) * inverse
        prob = weights * inverse
        grad_score = (prob * (grad_prob - offset)).astype(jnp.bfloat16)
        deliver(0, tile, h, dot(grad_score, keys, ((0,), (0,))) * scale)
        value_grad = dot(prob.astype(jnp.bfloat16), grads, ((1,), (0,)))
        key_grad = dot(grad_score, queries, ((1,), (0,))) * scale
        acc[h, 0, pl.ds(tile, 3)] += key_grad.reshape(3, BLOCK, HEAD_DIM)
        acc[h, 1, pl.ds(tile, 3)] += value_grad.reshape(3, BLOCK, HEAD_DIM)

    sib_slot = pl.multiple_of(TOKENS + core * CELL, CELL)
    far_rows = pl.ds(pl.multiple_of(far * CELL, CELL), CELL)
    out_rows = pl.ds(out_slot, CELL)

    def compute(h):
        beside(0, h).wait_recv()

        @pl.loop(1, GROUP - 1)
        def _(tile):
            tile_pass(tile, h)

        complete_edges(h)

        @pl.loop(0, 2)
        def _(edge):
            tile_pass((GROUP - 1) * edge, h)

        sib_from[h] = acc[h, :, :, pl.ds(sib_slot, CELL), :].astype(jnp.bfloat16)
        back_sib(h).start()

    def add_sibling(h):
        back_sib(h).wait_recv()
        acc[h, :, :, far_rows, :] += sib_to[h].astype(jnp.float32)
        for side, block, there in ((0, 0, has_left), (1, BLOCKS - 1, has_right)):
            @pl.when(there)
            def _():
                col_from[h, side, :, pl.ds(0, TOKENS), :] = acc[h, :, block, own_rows, :].astype(jnp.bfloat16)
                col_from[h, side, :, pl.ds(TOKENS, CELL), :] = acc[h, :, block, out_rows, :].astype(jnp.bfloat16)
                back_col(side, h).start()

    def add_sides(h):
        for side, block, there in ((0, GROUP, has_right), (1, 1, has_left)):
            @pl.when(there)
            def _():
                back_col(side, h).wait_recv()
                acc[h, :, block, own_rows, :] += col_to[h, side, :, pl.ds(0, TOKENS), :].astype(jnp.float32)
                acc[h, :, block, out_rows, :] += col_to[h, side, :, pl.ds(TOKENS, CELL), :].astype(jnp.float32)

        @pl.when(has_out)
        def _():
            for tile in range(GROUP):
                out_from[h, tile] = acc[h, :, tile + 1, out_rows, :].astype(jnp.bfloat16)
                back_out(tile, h).start()

        for tile in range(GROUP):
            for which in range(2):
                deliver(1 + which, tile, h, acc[h, which, tile + 1, own_rows, :])

    start_outer(0)
    start_share(0)
    start_outer(1)
    start_share(1)
    start_outer(2)
    start_share(2)
    setup()
    spread_own(0)
    spread_outer(0)
    spread_edges(0)
    spread_own(1)
    compute(0)
    spread_outer(1)
    spread_edges(1)
    spread_own(2)
    add_sibling(0)
    compute(1)
    add_sides(0)
    spread_outer(2)
    spread_edges(2)
    add_sibling(1)
    compute(2)
    add_sides(1)
    add_sibling(2)
    add_sides(2)

    for step in range(1, GROUP):
        remote(
            win.at[:, 1, own_rows, :], win.at[:, 1, own_rows, :],
            share_send.at[step], share_recv.at[step, 0], (row, first + lax.rem(x + step, GROUP)),
        ).wait_send()

    def sent(block, piece, sem, recv, device):
        remote(win.at[KV, block, piece, :], win.at[KV, block, piece, :], sem, recv, device).wait_send()

    @pl.when(has_out)
    def _():
        for step in range(GROUP):
            sent(1, pl.ds(out_slot, CELL), out_send.at[step], out_recv.at[step, 0], (outside, col))

    for kind in range(4):
        side = (has_left, has_right)[kind % 2]
        shift = (-GROUP, GROUP)[kind % 2]
        piece = own_rows if kind < 2 else pl.ds(out_slot, CELL)
        when(
            side if kind < 2 else both(side, has_out),
            lambda: sent(1, piece, col_send.at[kind], col_recv.at[kind, 0], (row, col + shift)),
        )
    for kind, count, there in ((0, GROUP, None), (1, 1, has_left), (2, 1, has_right)):
        piece = win.at[KV, pl.ds(0, count), pl.ds(0, CELL), :]
        when(there, lambda: remote(
            piece, piece, sib_send.at[kind], sib_recv.at[kind, 0], (sibling, col)
        ).wait_send())
    remote(sib_from, sib_to, back_sib_send.at[0], back_sib_recv.at[0], (sibling, col)).wait_send()
    for side, there in ((0, has_left), (1, has_right)):
        piece = col_from.at[:, side]
        when(there, lambda: remote(
            piece, piece, back_col_send.at[side], back_col_recv.at[side, 0], (row, col + (-GROUP, GROUP)[side])
        ).wait_send())
    pltpu.make_async_copy(parts.at[0], parts.at[0], part_local.at[0]).wait()
    for peer in range(GROUP):
        @pl.when(peer != x)
        def _():
            copy = remote(parts.at[peer], parts.at[peer], part_send.at[peer], part_recv.at[peer], (row, first + peer))
            copy.wait_send()
            copy.wait_recv()

    @pl.when(has_out)
    def _():
        for peer in range(GROUP):
            for h in range(per):
                remote(
                    out_from.at[h, 0], out_from.at[h, 0],
                    back_out_send.at[peer], back_out_recv.at[peer, h], (outside, col),
                ).wait_recv()
            remote(
                out_from.at[:, 0], out_from.at[:, 0],
                back_out_send.at[peer], back_out_recv.at[peer, 0], (outside, col),
            ).wait_send()
        edge = pl.ds(pl.multiple_of(core * CELL, CELL), CELL)
        for which in range(2):
            here = pl.ds((1 + which) * heads * HEAD_DIM, heads * HEAD_DIM)
            total = out_ref[edge, here].astype(jnp.float32) + out_to[which].astype(jnp.float32)
            out_ref[edge, here] = total.astype(jnp.bfloat16)


def per_device(queries, keys, values, out_grad):
    tile_rows, tile_cols, channels = queries.shape
    heads = channels // HEAD_DIM
    per = heads // GROUP
    rows, cols = lax.axis_size("row"), lax.axis_size("col")
    flat = [x.reshape(TOKENS, channels) for x in (queries, keys, values, out_grad)]
    dma = pltpu.SemaphoreType.DMA
    out = pl.pallas_call(
        functools.partial(kernel, heads, rows, cols),
        out_shape=jax.ShapeDtypeStruct((TOKENS, 3 * channels), jnp.bfloat16),
        in_specs=[pl.BlockSpec(memory_space=pl.ANY)] * 4,
        out_specs=pl.BlockSpec(memory_space=pltpu.VMEM),
        scratch_shapes=[
            pltpu.VMEM((4, TOKENS, channels), jnp.bfloat16),
            pltpu.VMEM((4, BLOCKS, BLOCK, per * HEAD_DIM), jnp.bfloat16),
            pltpu.VMEM((GROUP, SPAN, TOKENS), jnp.float32),
            pltpu.VMEM((per, 2, BLOCKS, BLOCK, HEAD_DIM), jnp.float32),
            pltpu.VMEM((per, 2, BLOCKS, CELL, HEAD_DIM), jnp.bfloat16),
            pltpu.VMEM((per, 2, BLOCKS, CELL, HEAD_DIM), jnp.bfloat16),
            pltpu.VMEM((per, 2, 2, TOKENS + CELL, HEAD_DIM), jnp.bfloat16),
            pltpu.VMEM((per, 2, 2, TOKENS + CELL, HEAD_DIM), jnp.bfloat16),
            pltpu.VMEM((per, GROUP, 2, CELL, HEAD_DIM), jnp.bfloat16),
            pltpu.VMEM((2, CELL, channels), jnp.bfloat16),
            pltpu.VMEM((GROUP, TOKENS, 3 * per * HEAD_DIM), jnp.bfloat16),
            dma((4,)),
            dma((per,)),
            dma((GROUP,)),
            dma((GROUP, per)),
            dma((GROUP,)),
            dma((GROUP, per)),
            dma((4,)),
            dma((4, per)),
            dma((3,)),
            dma((3, per)),
            dma((1,)),
            dma((per,)),
            dma((2,)),
            dma((2, per)),
            dma((GROUP,)),
            dma((GROUP, per)),
            dma((GROUP,)),
            dma((GROUP,)),
            dma((1,)),
        ],
        compiler_params=pltpu.CompilerParams(
            collective_id=0, has_side_effects=True, vmem_limit_bytes=60 * 1024 * 1024
        ),
        name="window_backward",
    )(*flat)
    return out.reshape(tile_rows, tile_cols, 3 * channels)


def solution(mesh):
    spec = P("row", "col", None)
    return jax.shard_map(
        per_device, mesh=mesh, in_specs=(spec,) * 4, out_specs=spec, check_vma=False
    )
```

time: 87.3 us -> 77.9 us (0.89)
  the two profiles are of different devices: /device:TPU:1 before, /device:TPU:15 now
where the time goes in v3:
time: 77.9 us; the launch traced here: 77.7 us
  Pallas kernels  75.4 us (97%)
  local copies, waits for them, and re-layouts  2.36 us (3%)
    pallas_call x1, Pallas kernels, per_device(): pl.pallas_call(functools.partial(kernel, heads, rows, cols), out_shape=ja...  75.4 us
    unnamed x1, local copies, waits for them, and re-layouts  2.36 us

profile of v3, /device:TPU:15, one launch (start us, length us, event | category | flops | bytes accessed | tf_op | source)
XLA Modules:
  0.0 77.7 jit_solution(14022699910569080122)
XLA Ops:
  0.0 75.4 %window_backward.1 = bf16[128,4608]{1,0:T(8,128)(2,1)} custom-call(bf16[128,1536]{1,0:T(8,128)(2,1)} %bitcast.6, bf16[128,1536]{1,0:T(8,128)(2,1)} %bitcast.7, bf16[128,1536]{1,0:T(8,128)(2,1)} %bitcast.8, bf16[128,1536]{1,0:T(8,128)(2,1)} %bitcast.9), custom_call_target="tpu_custom_call" | custom-call | tf_op jit(solution)/shard_map/window_backward/pallas_call | solution.py:435
  75.4 2.4 %copy.6 = bf16[16,8,4608]{2,1,0:T(8,128)(2,1)} copy(bf16[16,8,4608]{2,1,0:T(8,128)(2,1)} %bitcast.5) | data formatting | bytes 2359296

commit v4 on v3

--- a/solution.py
+++ b/solution.py
@@ -149,7 +149,7 @@
         return remote(
             mine.at[KV, pl.ds(pl.multiple_of(core * CELL, CELL), CELL), lanes(per * peer + h)],
             win.at[KV, x + 1, pl.ds(pl.multiple_of(TOKENS + core * CELL, CELL), CELL), lanes(h)],
-            out_send.at[step], out_recv.at[step, h], (outside, first + peer),
+            out_send.at[step, h], out_recv.at[step, h], (outside, first + peer),
         )
 
     def column(kind, h):
@@ -171,10 +171,12 @@
     def back_sib(h):
         return remote(sib_from.at[h], sib_to.at[h], back_sib_send.at[0], back_sib_recv.at[h], (sibling, col))
 
-    def back_col(side, h):
+    def back_col(side, part, h):
+        piece = (own_rows, pl.ds(TOKENS, CELL))[part]
+        kind = 2 * side + part
         return remote(
-            col_from.at[h, side], col_to.at[h, side],
-            back_col_send.at[side], back_col_recv.at[side, h], (row, col + (-GROUP, GROUP)[side]),
+            col_from.at[h, side, :, piece], col_to.at[h, side, :, piece],
+            back_col_send.at[kind], back_col_recv.at[kind, h], (row, col + (-GROUP, GROUP)[side]),
         )
 
     def back_out(tile, h):
@@ -193,6 +195,12 @@
         def _():
             for step in range(GROUP):
                 outer(step, h).start()
+
+    def left_outer(h):
+        @pl.when(has_out)
+        def _():
+            for step in range(GROUP):
+                outer(step, h).wait_send()
 
     def spread_own(h):
         for step in range(1, GROUP):
@@ -295,6 +303,9 @@
     far_rows = pl.ds(pl.multiple_of(far * CELL, CELL), CELL)
     out_rows = pl.ds(out_slot, CELL)
 
+    sides_from = ((0, 0, has_left), (1, BLOCKS - 1, has_right))
+    sides_to = ((0, GROUP, has_right), (1, 1, has_left))
+
     def compute(h):
         beside(0, h).wait_recv()
 
@@ -308,33 +319,46 @@
         def _(edge):
             tile_pass((GROUP - 1) * edge, h)
 
+        @pl.when(has_out)
+        def _():
+            for side, block, there in sides_from:
+                @pl.when(there)
+                def _():
+                    col_from[h, side, :, pl.ds(TOKENS, CELL), :] = acc[h, :, block, out_rows, :].astype(jnp.bfloat16)
+                    back_col(side, 1, h).start()
+            for tile in range(1, GROUP - 1):
+                out_from[h, tile] = acc[h, :, tile + 1, out_rows, :].astype(jnp.bfloat16)
+                back_out(tile, h).start()
+
         sib_from[h] = acc[h, :, :, pl.ds(sib_slot, CELL), :].astype(jnp.bfloat16)
         back_sib(h).start()
 
     def add_sibling(h):
         back_sib(h).wait_recv()
         acc[h, :, :, far_rows, :] += sib_to[h].astype(jnp.float32)
-        for side, block, there in ((0, 0, has_left), (1, BLOCKS - 1, has_right)):
+        for side, block, there in sides_from:
             @pl.when(there)
             def _():
-                col_from[h, side, :, pl.ds(0, TOKENS), :] = acc[h, :, block, own_rows, :].astype(jnp.bfloat16)
-                col_from[h, side, :, pl.ds(TOKENS, CELL), :] = acc[h, :, block, out_rows, :].astype(jnp.bfloat16)
-                back_col(side, h).start()
+                col_from[h, side, :, own_rows, :] = acc[h, :, block, own_rows, :].astype(jnp.bfloat16)
+                back_col(side, 0, h).start()
+
+    def add_outer(h):
+        @pl.when(has_out)
+        def _():
+            for side, block, there in sides_to:
+                @pl.when(there)
+                def _():
+                    back_col(side, 1, h).wait_recv()
+                    acc[h, :, block, out_rows, :] += col_to[h, side, :, pl.ds(TOKENS, CELL), :].astype(jnp.float32)
+                out_from[h, block - 1] = acc[h, :, block, out_rows, :].astype(jnp.bfloat16)
+                back_out(block - 1, h).start()
 
     def add_sides(h):
-        for side, block, there in ((0, GROUP, has_right), (1, 1, has_left)):
+        for side, block, there in sides_to:
             @pl.when(there)
             def _():
-                back_col(side, h).wait_recv()
-                acc[h, :, block, own_rows, :] += col_to[h, side, :, pl.ds(0, TOKENS), :].astype(jnp.float32)
-                acc[h, :, block, out_rows, :] += col_to[h, side, :, pl.ds(TOKENS, CELL), :].astype(jnp.float32)
-
-        @pl.when(has_out)
-        def _():
-            for tile in range(GROUP):
-                out_from[h, tile] = acc[h, :, tile + 1, out_rows, :].astype(jnp.bfloat16)
-                back_out(tile, h).start()
-
+                back_col(side, 0, h).wait_recv()
+                acc[h, :, block, own_rows, :] += col_to[h, side, :, own_rows, :].astype(jnp.float32)
         for tile in range(GROUP):
             for which in range(2):
                 deliver(1 + which, tile, h, acc[h, which, tile + 1, own_rows, :])
@@ -348,22 +372,27 @@
     setup()
     spread_own(0)
     spread_outer(0)
+    spread_own(1)
     spread_edges(0)
-    spread_own(1)
+    spread_outer(1)
     compute(0)
-    spread_outer(1)
+    spread_own(2)
     spread_edges(1)
-    spread_own(2)
+    spread_outer(2)
+    compute(1)
+    add_outer(0)
     add_sibling(0)
-    compute(1)
+    spread_edges(2)
+    compute(2)
+    add_outer(1)
+    add_sibling(1)
+    add_outer(2)
+    add_sibling(2)
     add_sides(0)
-    spread_outer(2)
-    spread_edges(2)
-    add_sibling(1)
-    compute(2)
     add_sides(1)
-    add_sibling(2)
     add_sides(2)
+    for h in range(per):
+        left_outer(h)
 
     for step in range(1, GROUP):
         remote(
@@ -373,11 +402,6 @@
 
     def sent(block, piece, sem, recv, device):
         remote(win.at[KV, block, piece, :], win.at[KV, block, piece, :], sem, recv, device).wait_send()
-
-    @pl.when(has_out)
-    def _():
-        for step in range(GROUP):
-            sent(1, pl.ds(out_slot, CELL), out_send.at[step], out_recv.at[step, 0], (outside, col))
 
     for kind in range(4):
         side = (has_left, has_right)[kind % 2]
@@ -393,11 +417,13 @@
             piece, piece, sib_send.at[kind], sib_recv.at[kind, 0], (sibling, col)
         ).wait_send())
     remote(sib_from, sib_to, back_sib_send.at[0], back_sib_recv.at[0], (sibling, col)).wait_send()
-    for side, there in ((0, has_left), (1, has_right)):
-        piece = col_from.at[:, side]
-        when(there, lambda: remote(
-            piece, piece, back_col_send.at[side], back_col_recv.at[side, 0], (row, col + (-GROUP, GROUP)[side])
-        ).wait_send())
+    for side, _, there in sides_from:
+        for part, cond in ((0, there), (1, there & has_out)):
+            piece = col_from.at[:, side, :, (own_rows, pl.ds(TOKENS, CELL))[part]]
+            when(cond, lambda: remote(
+                piece, piece, back_col_send.at[2 * side + part], back_col_recv.at[2 * side + part, 0],
+                (row, col + (-GROUP, GROUP)[side]),
+            ).wait_send())
     pltpu.make_async_copy(parts.at[0], parts.at[0], part_local.at[0]).wait()
     for peer in range(GROUP):
         @pl.when(peer != x)
@@ -453,7 +479,7 @@
             dma((per,)),
             dma((GROUP,)),
             dma((GROUP, per)),
-            dma((GROUP,)),
+            dma((GROUP, per)),
             dma((GROUP, per)),
             dma((4,)),
             dma((4, per)),
@@ -461,8 +487,8 @@
             dma((3, per)),
             dma((1,)),
             dma((per,)),
-            dma((2,)),
-            dma((2, per)),
+            dma((4,)),
+            dma((4, per)),
             dma((GROUP,)),
             dma((GROUP, per)),
             dma((GROUP,)),

time: 77.9 us -> 74.5 us (0.956)
  the two profiles are of different devices: /device:TPU:15 before, /device:TPU:39 now
where the time goes in v4:
time: 74.5 us; the launch traced here: 74.3 us
  Pallas kernels  72 us (97%)
  local copies, waits for them, and re-layouts  2.36 us (3%)
    pallas_call x1, Pallas kernels, per_device(): pl.pallas_call(functools.partial(kernel, heads, rows, cols), out_shape=ja...  72 us
    unnamed x1, local copies, waits for them, and re-layouts  2.36 us

profile of v4, /device:TPU:39, one launch (start us, length us, event | category | flops | bytes accessed | tf_op | source)
XLA Modules:
  0.0 74.3 jit_solution(10058025398739131142)
XLA Ops:
  0.0 72.0 %window_backward.1 = bf16[128,4608]{1,0:T(8,128)(2,1)} custom-call(bf16[128,1536]{1,0:T(8,128)(2,1)} %bitcast.6, bf16[128,1536]{1,0:T(8,128)(2,1)} %bitcast.7, bf16[128,1536]{1,0:T(8,128)(2,1)} %bitcast.8, bf16[128,1536]{1,0:T(8,128)(2,1)} %bitcast.9), custom_call_target="tpu_custom_call" | custom-call | tf_op jit(solution)/shard_map/window_backward/pallas_call | solution.py:461
  72.0 2.4 %copy.6 = bf16[16,8,4608]{2,1,0:T(8,128)(2,1)} copy(bf16[16,8,4608]{2,1,0:T(8,128)(2,1)} %bitcast.5) | data formatting | bytes 2359296

commit v5 on v4

--- a/solution.py
+++ b/solution.py
@@ -16,7 +16,7 @@
 CELL = 64
 BLOCK = 2 * TOKENS
 SPAN = 3 * BLOCK
-KV = pl.ds(1, 2)
+KV, QG = pl.ds(0, 2), pl.ds(2, 2)
 GROUP = 4
 BLOCKS = GROUP + 2
 FLOOR = -1e30
@@ -90,7 +90,7 @@
     has_left = group > 0
     has_right = group < cols // GROUP - 1
     loads = []
-    for a, ref in enumerate((q_ref, k_ref, v_ref, g_ref)):
+    for a, ref in enumerate((k_ref, v_ref, q_ref, g_ref)):
         copy = pltpu.make_async_copy(ref, mine.at[a], load_sem.at[a])
         copy.start()
         loads.append(copy)
@@ -132,11 +132,11 @@
             device_id=device, device_id_type=MESH,
         )
 
-    def share(step, h):
+    def share(step, h, part):
         peer = lax.rem(x + step, GROUP)
         return remote(
-            mine.at[:, :, lanes(per * peer + h)], win.at[:, x + 1, own_rows, lanes(h)],
-            share_send.at[step], share_recv.at[step, h], (row, first + peer),
+            mine.at[(KV, QG)[part], :, lanes(per * peer + h)], win.at[(KV, QG)[part], x + 1, own_rows, lanes(h)],
+            share_send.at[step], share_recv.at[step, 2 * h + part], (row, first + peer),
         )
 
     def keep(h):
@@ -185,10 +185,11 @@
             back_out_send.at[tile], back_out_recv.at[x, h], (outside, first + tile),
         )
 
-    def start_share(h):
-        keep(h).start()
+    def start_share(h, part):
+        if part == 0:
+            keep(h).start()
         for step in range(1, GROUP):
-            share(step, h).start()
+            share(step, h, part).start()
 
     def start_outer(h):
         @pl.when(has_out)
@@ -204,7 +205,7 @@
 
     def spread_own(h):
         for step in range(1, GROUP):
-            share(step, h).wait_recv()
+            share(step, h, 0).wait_recv()
         keep(h).wait()
         when(has_left, lambda: column(0, h).start())
         when(has_right, lambda: column(1, h).start())
@@ -283,13 +284,13 @@
             ).start()
 
     def tile_pass(tile, h):
-        keys = span(1, tile, h)
-        queries, grads = own(0, tile, h), own(3, tile, h)
+        keys = span(0, tile, h)
+        queries, grads = own(2, tile, h), own(3, tile, h)
         scores = dot(keys, queries, ((1,), (1,))) * scale2 + bias[tile]
         peak = jnp.max(scores, axis=0, keepdims=True)
         weights = jnp.exp2(scores - peak)
         inverse = 1.0 / jnp.sum(weights, axis=0, keepdims=True)
-        grad_prob = dot(span(2, tile, h), grads, ((1,), (1,)))
+        grad_prob = dot(span(1, tile, h), grads, ((1,), (1,)))
         offset = jnp.sum(weights * grad_prob, axis=0, keepdims=True) * inverse
         prob = weights * inverse
         grad_score = (prob * (grad_prob - offset)).astype(jnp.bfloat16)
@@ -308,6 +309,8 @@
 
     def compute(h):
         beside(0, h).wait_recv()
+        for step in range(1, GROUP):
+            share(step, h, 1).wait_recv()
 
         @pl.loop(1, GROUP - 1)
         def _(tile):
@@ -364,19 +367,22 @@
                 deliver(1 + which, tile, h, acc[h, which, tile + 1, own_rows, :])
 
     start_outer(0)
-    start_share(0)
+    start_share(0, 0)
     start_outer(1)
-    start_share(1)
+    start_share(1, 0)
     start_outer(2)
-    start_share(2)
+    start_share(2, 0)
+    start_share(0, 1)
+    start_share(1, 1)
+    start_share(2, 1)
     setup()
     spread_own(0)
+    spread_own(1)
     spread_outer(0)
-    spread_own(1)
+    spread_own(2)
     spread_edges(0)
     spread_outer(1)
     compute(0)
-    spread_own(2)
     spread_edges(1)
     spread_outer(2)
     compute(1)
@@ -478,7 +484,7 @@
             dma((4,)),
             dma((per,)),
             dma((GROUP,)),
-            dma((GROUP, per)),
+            dma((GROUP, 2 * per)),
             dma((GROUP, per)),
             dma((GROUP, per)),
             dma((4,)),

time: 74.5 us -> 73.9 us (level)
  the two profiles are of different devices: /device:TPU:39 before, /device:TPU:89 now
where the time goes in v5:
time: 73.9 us; the launch traced here: 73.8 us
  Pallas kernels  71.4 us (97%)
  local copies, waits for them, and re-layouts  2.36 us (3%)
    pallas_call x1, Pallas kernels, per_device(): pl.pallas_call(functools.partial(kernel, heads, rows, cols), out_shape=ja...  71.4 us
    unnamed x1, local copies, waits for them, and re-layouts  2.36 us

profile of v5, /device:TPU:89, one launch (start us, length us, event | category | flops | bytes accessed | tf_op | source)
XLA Modules:
  0.0 73.8 jit_solution(9228674638491753490)
XLA Ops:
  0.0 71.4 %window_backward.1 = bf16[128,4608]{1,0:T(8,128)(2,1)} custom-call(bf16[128,1536]{1,0:T(8,128)(2,1)} %bitcast.6, bf16[128,1536]{1,0:T(8,128)(2,1)} %bitcast.7, bf16[128,1536]{1,0:T(8,128)(2,1)} %bitcast.8, bf16[128,1536]{1,0:T(8,128)(2,1)} %bitcast.9), custom_call_target="tpu_custom_call" | custom-call | tf_op jit(solution)/shard_map/window_backward/pallas_call | solution.py:467
  71.4 2.4 %copy.6 = bf16[16,8,4608]{2,1,0:T(8,128)(2,1)} copy(bf16[16,8,4608]{2,1,0:T(8,128)(2,1)} %bitcast.5) | data formatting | bytes 2359296
